TPU v7x, 512 devices: a whole 4x8x8 slice. The times are simulated.
512 devices in a mesh: band: 8 (over z_hi, core), tile: 64 (over x, y, z_lo).
Axes of the slice: x: 4, y: 8, z: 8 (z_hi: 4, z_lo: 2; z = z_hi * 2 + z_lo), core: 2. Of those that a mesh axis runs over, the one named last changes fastest.
Arguments:
- waveforms: bfloat16 [2048, 32, 500], P('tile', 'band'), may hold values from -6 to 6
- band_widths: int32 [8], replicated, may hold values from 1 to 34, 180 in all
- pair_table: int32 [64, 33], P('tile'), may hold values from 0 to 63, as said below
Outputs:
- correlations: bfloat16 [64, 33, 32, 32, 51], P('tile', None, 'band')
Inputs may be any that keep to these rules, and one draw needn't show every extreme that they name: `band_widths`: the widths sum to 180; the largest is exactly 34. `pair_table`: row t lists the blocks t, t - 1, ..., t - 33 + 1 modulo 64, each once, in some order.
All inputs are finite; a program needn't handle non-finite values.
Results may differ from a plain program's by a relative error of at most 0.018.
Values may be sent and summed in bfloat16 or wider, within the bound.
A program may use at most 192 MiB of HBM per device.

v0:
```python
import math

import jax
import jax.numpy as jnp
from jax import lax
from jax.sharding import PartitionSpec as P

BINS = 180
FIRST = 20
LAGS = 51


EPS = 1e-05


def slot_bins(band_widths, capacity):
    offsets = jnp.cumsum(band_widths) - band_widths
    slot_ids = jnp.arange(capacity, dtype=jnp.int32)
    bin_freq = FIRST + offsets[:, None] + slot_ids[None, :]
    in_band = (slot_ids[None, :] < band_widths[:, None]).astype(jnp.float32)
    return (bin_freq, in_band)


def forward_table(bin_freq, in_band, sample_count):
    sample_ids = jnp.arange(sample_count, dtype=jnp.int32)
    phase_ids = sample_ids[:, None, None] * bin_freq[None] % sample_count
    angles = phase_ids.astype(jnp.float32) * (2.0 * math.pi / sample_count)
    weight = in_band[None]
    return jnp.stack([jnp.cos(angles) * weight, -jnp.sin(angles) * weight], axis=2).astype(
        jnp.bfloat16
    )


def inverse_table(bin_freq, in_band, sample_count, lag_count):
    lag_ids = jnp.arange(lag_count, dtype=jnp.int32) - lag_count // 2
    phase_ids = bin_freq[:, :, None] * lag_ids[None, None, :] % sample_count
    angles = phase_ids.astype(jnp.float32) * (2.0 * math.pi / sample_count)
    weight = in_band[:, :, None]
    return jnp.stack([jnp.cos(angles) * weight, -jnp.sin(angles) * weight], axis=1).astype(
        jnp.bfloat16
    )


def body(waveforms, band_widths, pair_table):
    block_rows, seg_local, sample_count = waveforms.shape
    band_count = lax.axis_size("band")
    tile_count = lax.axis_size("tile")
    capacity = (BINS + band_count - 1) // band_count + BINS // (2 * band_count)
    bin_freq, in_band = slot_bins(band_widths, capacity)
    forward = forward_table(bin_freq, in_band, sample_count).reshape(
        sample_count, band_count * 2 * capacity
    )
    spectra = jnp.dot(
        waveforms.reshape(block_rows * seg_local, sample_count),
        forward,
        preferred_element_type=jnp.float32,
    )
    spectra = spectra.astype(jnp.bfloat16).reshape(block_rows, seg_local, band_count, 2, capacity)
    banded = lax.all_to_all(spectra, "band", split_axis=2, concat_axis=1, tiled=True)
    seg_total = seg_local * band_count
    banded = banded.reshape(block_rows, seg_total, 2, capacity)
    my_band = lax.axis_index("band")
    my_width = lax.dynamic_index_in_dim(band_widths, my_band, 0, keepdims=False)
    values = banded.astype(jnp.float32)
    energy = jnp.sum(values * values, axis=(1, 2, 3)) / (seg_total * my_width.astype(jnp.float32))
    gain = lax.rsqrt(energy + EPS)
    whitened = (values * gain[:, None, None, None]).astype(jnp.bfloat16)
    own_cat = whitened.reshape(block_rows, seg_total * 2, capacity)
    own_alt = jnp.stack([whitened[:, :, 1], -whitened[:, :, 0]], axis=2).reshape(
        block_rows, seg_total * 2, capacity
    )
    partners = pair_table[0]
    slot_count = partners.shape[0]
    gathered = lax.all_gather(whitened, "tile", axis=0, tiled=True)
    gathered = gathered.reshape(tile_count, block_rows, seg_total, 2, capacity)
    selected = jnp.take(gathered, partners, axis=0).reshape(
        slot_count * block_rows, seg_total, 2, capacity
    )
    other_cat = selected.reshape(selected.shape[0], seg_total * 2, capacity)
    real_part = jnp.einsum("ixq,rxq->irq", own_cat, other_cat, preferred_element_type=jnp.float32)
    imag_part = jnp.einsum("ixq,rxq->irq", own_alt, other_cat, preferred_element_type=jnp.float32)
    grams = jnp.stack([real_part, imag_part], axis=2).reshape(
        block_rows, slot_count, block_rows, 2, capacity
    )
    cross_spec = jnp.transpose(grams, (1, 0, 2, 3, 4))
    inverse = inverse_table(bin_freq, in_band, sample_count, LAGS)
    my_inverse = lax.dynamic_index_in_dim(inverse, my_band, 0, keepdims=False).reshape(
        2 * capacity, LAGS
    )
    rounded = cross_spec.astype(jnp.bfloat16).reshape(
        slot_count * block_rows * block_rows, 2 * capacity
    )
    scale_out = 1.0 / math.sqrt(seg_total * BINS)
    partial_lags = jnp.dot(rounded, my_inverse, preferred_element_type=jnp.float32) * scale_out
    partial_lags = partial_lags.astype(jnp.bfloat16).astype(jnp.float32)
    partial_lags = partial_lags.reshape(slot_count, block_rows, block_rows, LAGS)
    summed = lax.psum_scatter(
        partial_lags.astype(jnp.bfloat16), "band", scatter_dimension=1, tiled=True
    )
    return summed[None]


def solution(mesh):
    placed = (P("tile", "band", None), P(), P("tile", None))
    return jax.shard_map(
        body,
        mesh=mesh,
        in_specs=placed,
        out_specs=P("tile", None, "band", None, None),
        check_vma=False,
    )
```

profile of v0, /device:TPU:1, one launch (start us, length us, event | category | flops | bytes accessed | tf_op | source)
XLA Modules:
  0.0 1179.6 jit_solution(15622617588086002054)
XLA Ops:
  6.5 0.8 fusion.23
  7.3 0.8 reduce-window.9
  8.2 0.7 fusion.25
  8.8 0.1 iota_add_fusion
  8.9 1.0 reshape.291
  9.9 3.2 multiply_convert_fusion.1
  13.1 0.1 pad_maximum_fusion
  13.2 0.3 convert_element_type.106
  13.4 0.3 fusion.9
  13.8 0.2 copy.15
  13.9 0.8 reshape.292
  14.7 0.4 copy.30
  15.1 1.6 reshape.312
  16.7 11.8 %all-to-all-start = ((bf16[8,2,4352]{2,1,0:T(2,128)(2,1)}), bf16[8,2,4352]{2,1,0:T(2,128)(2,1)S(1)}, u32[]{:S(2)}, u32[]{:S(2)}) async-start(bf16[8,2,4352]{2,1,0:T(2,128)(2,1)} %reshape.312), calls=%async_computation | async-start | bytes 278528 | tf_op jit(solution)/shard_map/all_to_all | solution.py:59
  28.5 0.6 dynamic_slice.8
  29.7 7.7 all-to-all-done
  37.4 1.4 reshape.313
  38.8 0.3 multiply_reduce_fusion
  39.1 0.1 copy_convert_fusion
  39.2 1.0 fusion.11
  40.2 0.0 all-reduce.3.cloned.1.call-start
  40.3 0.1 broadcast_in_dim.16
  40.4 0.1 broadcast_in_dim.17
  40.5 0.8 multiply_convert_fusion.2
  41.3 0.2 fusion.10
  41.5 0.8 copy.20
  42.3 1.1 fusion.28
  43.4 0.1 pad_maximum_fusion.1
  43.6 0.8 copy.21
  44.4 720.0 %all-gather.2.cloned.1.call-done = bf16[2048,32,2,34]{3,0,2,1:T(8,128)(2,1)} async-done(((bf16[32,32,2,34]{3,0,2,1:T(8,128)(2,1)}), bf16[2048,32,2,34]{3,0,2,1:T(8,128)(2,1)}) %all-gather.2.cloned.1.call-update) | async-done | bytes 8912912 | tf_op jit(solution)/shard_map/all_gather | solution.py:74
  764.4 29.4 %copy.18 = bf16[2048,32,2,34]{3,1,2,0:T(8,128)(2,1)} copy(bf16[2048,32,2,34]{3,0,2,1:T(8,128)(2,1)} %all-gather.2.cloned.1.call-done) | data formatting | bytes 17825792 | tf_op jit(solution)/shard_map/all_gather | solution.py:74
  793.8 14.9 %gather_fusion = bf16[33,32,32,2,34]{4,2,3,1,0:T(8,128)(2,1)} fusion(bf16[64,32,32,2,34]{4,2,3,1,0:T(8,128)(2,1)} %bitcast.65, s32[1024]{0:T(1024)S(1)} %pad_clamp_fusion), kind=kCustom, calls=%fused_computation | custom fusion | bytes 9191556 | tf_op jit(solution)/shard_map/jit(_take)/gather | solution.py:76
  808.7 49.2 %copy.19 = bf16[33,32,32,2,34]{1,0,3,2,4:T(8,128)(2,1)} copy(bf16[33,32,32,2,34]{4,2,3,1,0:T(8,128)(2,1)} %gather_fusion) | data formatting | bytes 9191424 | tf_op jit(solution)/shard_map/jit(_take)/gather | solution.py:76
  857.9 24.3 %gather.7 = bf16[1056,64,34]{0,1,2:T(8,128)(2,1)} reshape(bf16[33,32,32,2,34]{1,0,3,2,4:T(8,128)(2,1)} %copy.19) | data formatting | bytes 9191424 | tf_op jit(solution)/shard_map/jit(_take)/gather | solution.py:76
  882.1 3.6 fusion.5
  885.8 0.3 copy-done
  886.1 2.6 fusion.6
  888.6 12.5 %stack.28 = bf16[32,33,32,1,34]{2,1,0,4,3:T(8,128)(2,1)} reshape(bf16[32,1056,34]{1,0,2:T(8,128)(2,1)} %fusion.6) | data formatting | bytes 4595712 | tf_op jit(solution)/shard_map/stack | solution.py:82
  901.1 8.4 stack.26
  909.5 13.5 %maximum_bitcast_fusion = bf16[33,32,32,2,34]{2,0,1,4,3:T(8,128)(2,1)S(1)} fusion(bf16[32,33,32,1,34]{2,1,0,4,3:T(8,128)(2,1)} %stack.28, bf16[32,33,32,1,34]{2,1,0,4,3:T(8,128)(2,1)} %stack.26), kind=kLoop, calls=%fused_computation.3 | loop fusion | flops 2297856 | bytes 9191424 | tf_op jit(solution)/shard_map/convert_element_type | solution.py:90
  923.0 8.0 copy.22
  931.0 23.0 %reshape.295 = bf16[33792,68]{0,1:T(8,128)(2,1)} reshape(bf16[33,32,32,2,34]{2,1,0,4,3:T(8,128)(2,1)} %copy.22) | data formatting | bytes 9191424 | tf_op jit(solution)/shard_map/reshape | solution.py:90
  954.0 5.4 fusion
  959.4 8.7 copy.23
  968.1 0.0 all-reduce.3.cloned.1.call-update
  968.1 1.3 dynamic-slice
  970.1 200.2 %all-reduce.3.cloned.1.call-done = bf16[33,32,32,51]{3,2,1,0:T(8,128)(2,1)} async-done(((bf16[33,32,32,51]{3,2,1,0:T(8,128)(2,1)}), bf16[33,32,32,51]{3,2,1,0:T(8,128)(2,1)}) %all-reduce.3.cloned.1.call-update) | async-done | bytes 3446800
  1170.2 2.5 dynamic-slice_bitcast_fusion
  (14 shorter events, 0.1 us)
Async XLA Ops:
  6.5 22.0 %copy-start.1 = (s32[8]{0:T(128)S(1)}, s32[8]{0:T(128)}, u32[]{:S(2)}) copy-start(s32[8]{0:T(128)} %param.4) | copy-start | bytes 100
  13.2 27.1 %copy-start.2 = (s32[1,33]{1,0:T(1,128)S(1)}, s32[1,33]{1,0:T(1,128)}, u32[]{:S(2)}) copy-start(s32[1,33]{1,0:T(1,128)} %param.5) | copy-start | bytes 400
  16.7 20.7 %all-to-all-start = ((bf16[8,2,4352]{2,1,0:T(2,128)(2,1)}), bf16[8,2,4352]{2,1,0:T(2,128)(2,1)S(1)}, u32[]{:S(2)}, u32[]{:S(2)}) async-start(bf16[8,2,4352]{2,1,0:T(2,128)(2,1)} %reshape.312), calls=%async_computation | async-start | bytes 278528 | tf_op jit(solution)/shard_map/all_to_all | solution.py:59
  28.5 735.9 %all-gather.2.cloned.1.call-start = ((), (), s32[]{:S(2)}) async-start(), calls=%async_computation.1 | async-start | bytes 34078720 | tf_op jit(solution)/shard_map/all_gather | solution.py:74
  40.2 1130.0 %all-reduce.3.cloned.1.call-start = ((), (), s32[]{:S(2)}) async-start(), calls=%async_computation.2 | async-start | bytes 17301504
  882.1 3.9 copy-start
Sparse Core Ops, SparseCore 0:
  40.4 724.0 all-gather.1
  968.2 201.9 all-reduce.2
where the time goes:
time: 1190 us; the launch traced here: 1180 us
  waiting for transfers between devices  928 us (78%)
  local copies, waits for them, and re-layouts  190 us (16%)
  other arithmetic  22.7 us (2%)
  between operations  14.8 us (1%)
  matrix products  11.9 us (1%)
    all_gather x1, waiting for transfers between devices, body(): gathered = lax.all_gather(whitened, 'tile', axis=0, tiled=True)  720 us
    unnamed x3, waiting for transfers between devices  200 us
    gather x3, local copies, waits for them, and re-layouts, body(): jnp.take(gathered, partners, axis=0)  88.3 us
    all_gather x1, local copies, waits for them, and re-layouts, body(): gathered = lax.all_gather(whitened, 'tile', axis=0, tiled=True)  29.4 us
  transfers between devices with their start and end apart: 3, of which 3 were waited for; matrix products, arithmetic and copies ran while one was open for 0% of the time, Pallas kernels for 0%

commit v1 on v0

v1 whole, which is shorter than its diff:
```python
import functools
import math

import jax
import jax.numpy as jnp
import ml_dtypes
import numpy as np
from jax import lax
from jax.experimental import pallas as pl
from jax.experimental.pallas import tpu as pltpu
from jax.sharding import PartitionSpec as P

BINS = 180
FIRST = 20
LAGS = 51
SAMPLES = 500
EPS = 1e-05

BAND = 8
TILE = 64
CH = 32
SEG = 32
SEGL = 4
QN = 24
GROUPS = QN // 4
ROWS = 2 * QN
WIDE = QN * 64
PART = 208
HALF_A = 112
SCALE = 1.0 / math.sqrt(SEG * BINS)
MESH = pl.DeviceIdType.MESH

ORDER = [0, 8, 16, 1, 9, 7, 15, 2, 10, 6, 14, 3, 11, 5, 13, 4, 12]
POS = {r: i for i, r in enumerate(ORDER)}
CHUNKS = [(0, 256), (256, 256), (512, 256), (768, 256), (1024, 128)]
JALL = 1152


def _forward_const():
    n = np.arange(SAMPLES)
    table = np.zeros((BAND * QN, 2, 512), np.float32)
    for k in range(BINS):
        angle = ((n * (FIRST + k)) % SAMPLES) * (2.0 * math.pi / SAMPLES)
        table[k, 0, :SAMPLES] = np.cos(angle)
        table[k, 1, :SAMPLES] = -np.sin(angle)
    return table.reshape(BAND * ROWS, 512).astype(ml_dtypes.bfloat16)


def _inverse_const():
    tau = np.arange(LAGS) - LAGS // 2
    table = np.zeros((BAND * QN, 2, LAGS), np.float32)
    for k in range(BINS):
        angle = (((FIRST + k) * tau) % SAMPLES) * (2.0 * math.pi / SAMPLES)
        table[k, 0] = np.cos(angle)
        table[k, 1] = -np.sin(angle)
    table = table.reshape(BAND, GROUPS, 4, 2, LAGS)
    out = np.zeros((BAND, 4, PART, GROUPS, 4, 2, 16), np.float32)
    for b4 in range(4):
        for i4 in range(4):
            rows = np.moveaxis(table, -1, 1)
            out[:, b4, i4 * LAGS : (i4 + 1) * LAGS, :, :, :, b4 * 4 + i4] = rows
    return out.reshape(BAND, 4 * PART, GROUPS * 128).astype(ml_dtypes.bfloat16)


def _select_const():
    out = np.zeros((PART, 512), np.float32)
    for i4 in range(4):
        for lag in range(LAGS):
            out[i4 * LAGS + lag, i4 * 128 + lag] = 1.0
    return out.astype(ml_dtypes.bfloat16)


def _main_kernel(widths, wave, fwd, inv_all, out, *scratch):
    sb, rb, g, wt, kt, ct = scratch[:6]
    bufs = [scratch[6 + 6 * k : 12 + 6 * k] for k in range(len(CHUNKS))]
    (kt_sem, a_send, a_recv, g_send, g_recv, r_send, r_recv) = scratch[6 + 6 * len(CHUNKS) :]
    f32, bf16 = jnp.float32, jnp.bfloat16

    band = lax.axis_index("band")
    tile = lax.axis_index("tile")
    core = lax.rem(band, 2)
    zh = band // 2
    z = lax.rem(tile, 2)

    def at_band(b):
        return {"band": b, "tile": tile}

    def at_tile(t):
        return {"band": band, "tile": lax.rem(t + TILE, TILE)}

    barrier = pltpu.get_barrier_semaphore()
    peers = [at_band(lax.rem(band + o, BAND)) for o in range(1, BAND)]
    other_z = tile + 1 - 2 * z
    peers += [at_tile(other_z)] + [at_tile(tile + d) for d in (16, -16, 32, 2, -2)]
    for peer in peers:
        pl.semaphore_signal(barrier, inc=1, device_id=peer, device_id_type=MESH)
    kt_copy = pltpu.make_async_copy(inv_all.at[band], kt, kt_sem)
    kt_copy.start()

    nt = (((1,), (1,)), ((), ()))
    spectra = lax.dot_general(fwd[...], wave[...], nt, preferred_element_type=f32).astype(bf16)
    values = spectra.astype(f32)
    squares = values * values
    sq_hi = squares.astype(bf16)
    sq_lo = (squares - sq_hi.astype(f32)).astype(bf16)
    offsets = []
    total = widths[0] * 0
    for b in range(BAND):
        offsets.append(total)
        total = total + widths[b]

    def member(rows, bins):
        low = jnp.zeros(rows.shape, jnp.int32)
        size = jnp.zeros(rows.shape, jnp.int32)
        for b in range(BAND):
            low = jnp.where(rows == b, offsets[b], low)
            size = jnp.where(rows == b, widths[b], size)
        return jnp.where((bins >= low) & (bins < low + size), 1.0, 0.0).astype(f32)

    shape = (BAND, BAND * ROWS)
    is_in = member(
        lax.broadcasted_iota(jnp.int32, shape, 0), lax.broadcasted_iota(jnp.int32, shape, 1) // 2
    ).astype(bf16)
    part = jnp.dot(is_in, sq_hi, preferred_element_type=f32)
    part = part + jnp.dot(is_in, sq_lo, preferred_element_type=f32)
    part_hi = part.astype(bf16).astype(f32)
    energies = jnp.concatenate([part_hi, part - part_hi], axis=0).astype(bf16)
    for b in range(BAND):
        sb[b, :ROWS] = spectra[b * ROWS : (b + 1) * ROWS]
        sb[b, ROWS:] = energies
    g[1088:, :] = jnp.zeros((JALL - 1088, WIDE), bf16)
    rb[0] = sb[band]

    pl.semaphore_wait(barrier, len(peers))

    exchange = []
    for o in range(1, BAND):
        to = lax.rem(band + o, BAND)
        copy = pltpu.make_async_remote_copy(
            src_ref=sb.at[to],
            dst_ref=rb.at[o],
            send_sem=a_send.at[o],
            recv_sem=a_recv.at[o],
            device_id=at_band(to),
            device_id_type=MESH,
        )
        copy.start()
        exchange.append(copy)
    for copy in exchange:
        copy.wait_recv()

    energy = jnp.zeros((BAND, 128), f32)
    for o in range(BAND):
        tail = rb[o, ROWS:].astype(f32)
        energy = energy + tail[:BAND] + tail[BAND:]
    energy = energy + pltpu.roll(energy, 64, 1)
    energy = energy + pltpu.roll(energy, 32, 1)
    row8 = lax.broadcasted_iota(jnp.int32, (BAND, 128), 0)
    width8 = jnp.ones((BAND, 128), f32)
    for b in range(BAND):
        width8 = jnp.where(row8 == b, widths[b].astype(f32), width8)
    gain = lax.rsqrt(energy / (SEG * width8) + EPS)
    bins = band * QN + lax.broadcasted_iota(jnp.int32, (ROWS, 128), 0) // 2
    gains = jnp.zeros((ROWS, 128), f32)
    for b in range(BAND):
        inside = (bins >= offsets[b]) & (bins < offsets[b] + widths[b])
        gains = jnp.where(inside, gain[b : b + 1, :], gains)
    white = [(rb[o, :ROWS].astype(f32) * gains).astype(bf16).astype(f32) for o in range(BAND)]

    lane = lax.broadcasted_iota(jnp.int32, (CH, 128), 1)
    own_row = pl.multiple_of(z * CH, CH)
    tiles = []
    for pair in range(GROUPS // 2):
        stack = jnp.concatenate(
            [white[o][(2 * pair + h) * 8 : (2 * pair + h + 1) * 8] for h in range(2) for o in range(BAND)],
            axis=0,
        )
        flipped = jnp.transpose(stack)
        rolled = pltpu.roll(flipped, 64, 1)
        seg = [flipped[s * CH : (s + 1) * CH] for s in range(SEGL)]
        seg_r = [rolled[s * CH : (s + 1) * CH] for s in range(SEGL)]
        for h in range(2):
            low, high = (seg, seg_r) if h == 0 else (seg_r, seg)
            halves = [jnp.where(lane < 64, low[2 * v], high[2 * v + 1]) for v in range(2)]
            tiles.append(halves)
            base = (2 * pair + h) * 256
            for v in range(2):
                g[pl.ds(own_row, CH), base + v * 128 : base + (v + 1) * 128] = halves[v].astype(bf16)

    def slot(r, half=None):
        if half is None:
            return g.at[pl.ds(POS[r] * 64, 64)]
        return g.at[pl.ds(pl.multiple_of(POS[r] * 64 + half * CH, CH), CH)]

    copies = {}

    def move(name, src, dst, to):
        n = len(copies)
        copy = pltpu.make_async_remote_copy(
            src_ref=src,
            dst_ref=dst,
            send_sem=g_send.at[n],
            recv_sem=g_recv.at[n],
            device_id=at_tile(to),
            device_id_type=MESH,
        )
        copy.start()
        copies[name] = copy

    move("z", slot(0, z), slot(0, z), other_z)
    move("x1", slot(0, z), slot(8, z), tile + 16)
    move("x2", slot(0, z), slot(16, z), tile + 32)

    even = lax.rem(lane, 2) == 0
    bin4 = lax.rem(lane // 2, 4)
    for n, halves in enumerate(tiles):
        for v in range(2):
            own = halves[v]
            alt = jnp.where(even, pltpu.roll(own, 127, 1), -pltpu.roll(own, 1, 1))
            for q in range(4):
                for p in range(2):
                    kept = jnp.where(bin4 == q, own if p == 0 else alt, 0.0).astype(bf16)
                    for h in range(2):
                        row = h * 128 + q * 32 + p * 16
                        wt[n, row : row + 16, v * 128 : (v + 1) * 128] = kept[h * 16 : h * 16 + 16]

    def forward(kind, k):
        if kind == "fa":
            src, dst, to = k - 1, k, tile + 2
        elif kind == "fb":
            src, dst, to = 8 + k - 1, 8 + k, tile + 2
        elif kind == "ba":
            src, dst, to = 8 - (k - 1), 8 - k, tile - 2
        else:
            src, dst, to = 16 - (k - 1), 16 - k, tile - 2
        move(kind + str(k), slot(src), slot(dst), to)

    def arrive(kind, k, last):
        copies[kind + str(k)].wait_recv()
        if k < last:
            forward(kind, k + 1)

    copies["z"].wait_recv()
    move("x1s", slot(0, 1 - z), slot(8, 1 - z), tile + 16)
    move("x2s", slot(0, 1 - z), slot(16, 1 - z), tile + 32)
    forward("fa", 1)
    copies["x1"].wait_recv()
    copies["x1s"].wait_recv()
    forward("ba", 1)
    forward("fb", 1)
    copies["x2"].wait_recv()
    copies["x2s"].wait_recv()
    forward("bb", 1)

    def compute(k):
        start, size = CHUNKS[k]
        mine = bufs[k][0]
        for n in range(GROUPS):
            block = g[start : start + size, n * 256 : (n + 1) * 256]
            cross = lax.dot_general(wt[n], block, nt, preferred_element_type=f32).astype(bf16)
            for h in range(2):
                ct[h, n * 128 : (n + 1) * 128, :size] = cross[h * 128 : (h + 1) * 128]
        for h in range(2):
            lags = jnp.dot(kt[...], ct[h, :, :size], preferred_element_type=f32) * SCALE
            for b4 in range(4):
                mine[b4 % 2, 2 * h + b4 // 2] = lags[b4 * PART : (b4 + 1) * PART].astype(bf16)

    sums = {}

    def send(name, n, k, src, dst, to):
        copy = pltpu.make_async_remote_copy(
            src_ref=src,
            dst_ref=dst,
            send_sem=r_send.at[k * 5 + n],
            recv_sem=r_recv.at[k * 5 + n],
            device_id=at_band(to),
            device_id_type=MESH,
        )
        copy.start()
        sums[(name, k)] = copy

    up, down, far = lax.rem(zh + 1, 4), lax.rem(zh + 3, 4), lax.rem(zh + 2, 4)
    to_sibling, to_up, to_down = 2 * zh + 1 - core, 2 * up + core, 2 * down + core

    def r0(k):
        compute(k)
        send("sib", 0, k, bufs[k][0].at[1 - core], bufs[k][1], to_sibling)

    def r1(k):
        mine, theirs, both, h1, h2, _ = bufs[k]
        sums[("sib", k)].wait_recv()
        for n in (far, up, down, zh):
            both[n] = (mine[core, n].astype(f32) + theirs[n].astype(f32)).astype(bf16)
            if n is far:
                send("ha", 1, k, both.at[far, pl.ds(0, HALF_A)], h1, to_up)
                send("hb", 2, k, both.at[far, pl.ds(HALF_A, PART - HALF_A)], h2, to_down)

    def r2(k):
        _, _, both, h1, h2, final = bufs[k]
        sums[("ha", k)].wait_recv()
        both[up, :HALF_A] = (both[up, :HALF_A].astype(f32) + h1[...].astype(f32)).astype(bf16)
        send("fu", 3, k, both.at[up], final.at[0], to_up)
        sums[("hb", k)].wait_recv()
        both[down, HALF_A:] = (both[down, HALF_A:].astype(f32) + h2[...].astype(f32)).astype(bf16)
        send("fd", 4, k, both.at[down], final.at[1], to_down)

    def r3(k):
        _, _, both, _, _, final = bufs[k]
        start, size = CHUNKS[k]
        sums[("fu", k)].wait_recv()
        sums[("fd", k)].wait_recv()
        whole = both[zh].astype(f32) + final[0].astype(f32) + final[1].astype(f32)
        out[:, start : start + size] = whole.astype(bf16)

    kt_copy.wait()
    arrive("fa", 1, 4)
    arrive("ba", 1, 3)
    r0(0)
    arrive("fb", 1, 3)
    arrive("bb", 1, 4)
    r1(0)
    arrive("fa", 2, 4)
    arrive("ba", 2, 3)
    r0(1)
    r2(0)
    arrive("fb", 2, 3)
    arrive("bb", 2, 4)
    r1(1)
    arrive("fa", 3, 4)
    arrive("ba", 3, 3)
    r0(2)
    r2(1)
    r3(0)
    arrive("fb", 3, 3)
    arrive("bb", 3, 4)
    r1(2)
    arrive("fa", 4, 4)
    arrive("bb", 4, 4)
    r0(3)
    r2(2)
    r1(3)
    r0(4)
    r3(1)
    r2(3)
    r1(4)
    r3(2)
    r2(4)
    r3(3)
    r3(4)

    for copy in exchange:
        copy.wait_send()
    for copy in copies.values():
        copy.wait_send()
    for copy in sums.values():
        copy.wait_send()


def _place_kernel(table, place, summed, select, out, turned):
    tile = lax.axis_index("tile")
    rows = lax.dot_general(
        summed[...], select[...], (((0,), (0,)), ((), ())), preferred_element_type=jnp.float32
    )
    turned[...] = rows.astype(jnp.bfloat16).reshape(turned.shape)

    def step(s, carry):
        partner = table[0, s]
        behind = lax.rem(tile // 2 - partner // 2 + TILE // 2, TILE // 2)
        block = place[behind] * 2 + lax.rem(partner, 2)
        for i4 in range(4):
            out[s, i4] = turned[block, :, i4 * 128 : i4 * 128 + LAGS]
        return carry

    lax.fori_loop(0, out.shape[0], step, 0)


def body(waveforms, band_widths, pair_table):
    slots = pair_table.shape[1]
    wave = jnp.transpose(waveforms, (1, 0, 2)).reshape(SEGL * CH, SAMPLES)
    wave = jnp.pad(wave, ((0, 0), (0, 512 - SAMPLES)))
    bf16 = jnp.bfloat16
    scratch = [
        pltpu.VMEM((BAND, 64, 128), bf16),
        pltpu.VMEM((BAND, 64, 128), bf16),
        pltpu.VMEM((JALL, WIDE), bf16),
        pltpu.VMEM((GROUPS, 256, 256), bf16),
        pltpu.VMEM((4 * PART, GROUPS * 128), bf16),
        pltpu.VMEM((2, GROUPS * 128, 256), bf16),
    ]
    for _, size in CHUNKS:
        scratch += [
            pltpu.VMEM((2, 4, PART, size), bf16),
            pltpu.VMEM((4, PART, size), bf16),
            pltpu.VMEM((4, PART, size), bf16),
            pltpu.VMEM((HALF_A, size), bf16),
            pltpu.VMEM((PART - HALF_A, size), bf16),
            pltpu.VMEM((2, PART, size), bf16),
        ]
    dma = pltpu.SemaphoreType.DMA
    scratch += [
        dma,
        dma((BAND,)),
        dma((BAND,)),
        dma((19,)),
        dma((19,)),
        dma((5 * len(CHUNKS),)),
        dma((5 * len(CHUNKS),)),
    ]
    vmem = pl.BlockSpec(memory_space=pltpu.VMEM)
    smem = pl.BlockSpec(memory_space=pltpu.SMEM)
    summed = pl.pallas_call(
        _main_kernel,
        out_shape=jax.ShapeDtypeStruct((PART, JALL), bf16),
        in_specs=[smem, vmem, vmem, pl.BlockSpec(memory_space=pl.ANY)],
        out_specs=vmem,
        scratch_shapes=scratch,
        compiler_params=pltpu.CompilerParams(
            collective_id=0, has_side_effects=True, vmem_limit_bytes=40 * 1024 * 1024
        ),
        name="correlate",
    )(band_widths, wave, jnp.asarray(_forward_const()), jnp.asarray(_inverse_const()))
    place = np.zeros((TILE // 2,), np.int32)
    for r, i in POS.items():
        place[r] = i
    placed = pl.pallas_call(
        _place_kernel,
        out_shape=jax.ShapeDtypeStruct((slots, 4, CH, LAGS), bf16),
        in_specs=[smem, smem, vmem, vmem],
        out_specs=vmem,
        scratch_shapes=[pltpu.VMEM((JALL // CH, CH, 512), bf16)],
        compiler_params=pltpu.CompilerParams(vmem_limit_bytes=32 * 1024 * 1024),
        name="place",
    )(pair_table, jnp.asarray(place), summed, jnp.asarray(_select_const()))
    return placed[None]


def solution(mesh):
    placed = (P("tile", "band", None), P(), P("tile", None))
    return jax.shard_map(
        body,
        mesh=mesh,
        in_specs=placed,
        out_specs=P("tile", None, "band", None, None),
        check_vma=False,
    )
```

time: 1190 us -> 111 us (0.09)
  the two profiles are of different devices: /device:TPU:1 before, /device:TPU:68 now
where the time goes in v1:
time: 111 us
  Pallas kernels  105 us (95%)
  local copies, waits for them, and re-layouts  6.55 us (6%)
    pallas_call x1, Pallas kernels, body(): pl.pallas_call(_main_kernel, out_shape=jax.ShapeDtypeStruct((PART, JALL),...  102 us
    unnamed x12, local copies, waits for them, and re-layouts  5.56 us
    pallas_call x1, Pallas kernels, body(): pl.pallas_call(_place_kernel, out_shape=jax.ShapeDtypeStruct((slots, 4, C...  2.98 us

profile of v1, /device:TPU:68, one launch (start us, length us, event | category | flops | bytes accessed | tf_op | source)
XLA Modules:
  0.0 111.3 jit_solution(2878166369442369117)
XLA Ops:
  0.0 0.0 copy-start.2
  0.0 0.0 copy-start.4
  0.0 0.0 copy-start.3
  0.0 1.0 copy.8
  1.0 0.0 copy-start
  1.0 3.9 %copy-done = bf16[8,832,768]{2,1,0:T(8,128)(2,1)S(1)} copy-done((bf16[8,832,768]{2,1,0:T(8,128)(2,1)S(1)}, bf16[8,832,768]{2,1,0:T(8,128)(2,1)}, u32[]{:S(2)}) %copy-start) | copy-done | bytes 10223640
  4.9 0.0 copy-start.1
  4.9 1.0 copy-done.1
  5.9 0.0 copy-start.5
  5.9 0.7 copy-done.5
  6.6 101.7 %correlate.1.summed = bf16[208,1152]{1,0:T(8,128)(2,1)S(1)} custom-call(s32[8]{0:T(128)S(1)} %copy-done.5, bf16[128,512]{1,0:T(8,128)(2,1)S(1)} %pad.4.wave, bf16[384,512]{1,0:T(8,128)(2,1)S(1)} %copy-done.1, bf16[8,832,768]{2,1,0:T(8,128)(2,1)S(1)} %copy-done), custom_call_target="tpu_custom_call" | custom-call | tf_op jit(solution)/shard_map/correlate/pallas_call | solution.py:411
  108.2 0.0 copy-done.2
  108.3 0.0 copy-done.4
  108.3 0.0 copy-done.3
  108.3 3.0 %place.2 = bf16[33,4,32,51]{3,2,1,0:T(8,128)(2,1)} custom-call(s32[1,33]{1,0:T(1,128)S(1)} %copy-done.3, s32[32]{0:T(128)S(1)} %copy-done.4, bf16[208,1152]{1,0:T(8,128)(2,1)S(1)} %correlate.1.summed, bf16[208,512]{1,0:T(8,128)(2,1)S(1)} %copy-done.2), custom_call_target="tpu_custom_call" | custom-call | tf_op jit(solution)/shard_map/place/pallas_call | solution.py:425
  (1 shorter events, 0.0 us)
Async XLA Ops:
  0.0 108.3 %copy-start.2 = (bf16[208,512]{1,0:T(8,128)(2,1)S(1)}, bf16[208,512]{1,0:T(8,128)(2,1)}, u32[]{:S(2)}) copy-start(bf16[208,512]{1,0:T(8,128)(2,1)} %constant.14.clone.select) | copy-start | bytes 638980
  0.0 108.3 %copy-start.4 = (s32[32]{0:T(128)S(1)}, s32[32]{0:T(128)}, u32[]{:S(2)}) copy-start(s32[32]{0:T(128)} %constant.13.clone.place) | copy-start | bytes 388
  0.0 108.3 %copy-start.3 = (s32[1,33]{1,0:T(1,128)S(1)}, s32[1,33]{1,0:T(1,128)}, u32[]{:S(2)}) copy-start(s32[1,33]{1,0:T(1,128)} %table.1) | copy-start | bytes 400
  1.0 3.9 %copy-start = (bf16[8,832,768]{2,1,0:T(8,128)(2,1)S(1)}, bf16[8,832,768]{2,1,0:T(8,128)(2,1)}, u32[]{:S(2)}) copy-start(bf16[8,832,768]{2,1,0:T(8,128)(2,1)} %constant.12.clone.inv_all) | copy-start | bytes 30670852
  4.9 1.0 copy-start.1
  5.9 0.7 copy-start.5

commit v2 on v1

--- a/solution.py
+++ b/solution.py
@@ -30,20 +30,20 @@
 SCALE = 1.0 / math.sqrt(SEG * BINS)
 MESH = pl.DeviceIdType.MESH
 
-ORDER = [0, 8, 16, 1, 9, 7, 15, 2, 10, 6, 14, 3, 11, 5, 13, 4, 12]
+ORDER = [0, 8, 16, 1, 7, 9, 15, 2, 6, 10, 14, 3, 5, 11, 13, 4, 12]
 POS = {r: i for i, r in enumerate(ORDER)}
-CHUNKS = [(0, 256), (256, 256), (512, 256), (768, 256), (1024, 128)]
-JALL = 1152
+CHUNKS = 9
+JALL = 128 * CHUNKS
 
 
 def _forward_const():
     n = np.arange(SAMPLES)
-    table = np.zeros((BAND * QN, 2, 512), np.float32)
+    table = np.zeros((BAND * QN, 2, SAMPLES), np.float32)
     for k in range(BINS):
         angle = ((n * (FIRST + k)) % SAMPLES) * (2.0 * math.pi / SAMPLES)
-        table[k, 0, :SAMPLES] = np.cos(angle)
-        table[k, 1, :SAMPLES] = -np.sin(angle)
-    return table.reshape(BAND * ROWS, 512).astype(ml_dtypes.bfloat16)
+        table[k, 0] = np.cos(angle)
+        table[k, 1] = -np.sin(angle)
+    return table.reshape(BAND * ROWS, SAMPLES).astype(ml_dtypes.bfloat16)
 
 
 def _inverse_const():
@@ -70,10 +70,9 @@
     return out.astype(ml_dtypes.bfloat16)
 
 
-def _main_kernel(widths, wave, fwd, inv_all, out, *scratch):
-    sb, rb, g, wt, kt, ct = scratch[:6]
-    bufs = [scratch[6 + 6 * k : 12 + 6 * k] for k in range(len(CHUNKS))]
-    (kt_sem, a_send, a_recv, g_send, g_recv, r_send, r_recv) = scratch[6 + 6 * len(CHUNKS) :]
+def _main_kernel(widths_hbm, wave_hbm, fwd_hbm, inv_all, out, *scratch):
+    widths, wave, fwd, sb, rb, g, wt, kt, ct, parts, theirs, sums, h1, h2, final = scratch[:15]
+    (in_sem, a_send, a_recv, g_send, g_recv, r_send, r_recv) = scratch[15:]
     f32, bf16 = jnp.float32, jnp.bfloat16
 
     band = lax.axis_index("band")
@@ -81,6 +80,9 @@
     core = lax.rem(band, 2)
     zh = band // 2
     z = lax.rem(tile, 2)
+    y = lax.rem(tile // 2, 8)
+    first = (7 - y) // 7
+    last = (y + 1) // 8
 
     def at_band(b):
         return {"band": b, "tile": tile}
@@ -91,14 +93,25 @@
     barrier = pltpu.get_barrier_semaphore()
     peers = [at_band(lax.rem(band + o, BAND)) for o in range(1, BAND)]
     other_z = tile + 1 - 2 * z
-    peers += [at_tile(other_z)] + [at_tile(tile + d) for d in (16, -16, 32, 2, -2)]
+    above, below = tile + 2 - 16 * last, tile - 2 + 16 * first
+    peers += [at_tile(t) for t in (other_z, tile + 16, tile - 16, tile + 32)]
+    peers += [at_tile(t) for t in (tile + 2, tile - 2, above, below)]
     for peer in peers:
         pl.semaphore_signal(barrier, inc=1, device_id=peer, device_id_type=MESH)
-    kt_copy = pltpu.make_async_copy(inv_all.at[band], kt, kt_sem)
-    kt_copy.start()
+    wave_copy = pltpu.make_async_copy(wave_hbm, wave, in_sem.at[0])
+    fwd_copy = pltpu.make_async_copy(fwd_hbm, fwd, in_sem.at[1])
+    widths_copy = pltpu.make_async_copy(widths_hbm, widths, in_sem.at[2])
+    kt_copy = pltpu.make_async_copy(inv_all.at[band], kt, in_sem.at[3])
+    for copy in (wave_copy, fwd_copy, widths_copy, kt_copy):
+        copy.start()
+    g[1088:, :] = jnp.zeros((JALL - 1088, WIDE), bf16)
+    wave_copy.wait()
+    fwd_copy.wait()
+    widths_copy.wait()
 
     nt = (((1,), (1,)), ((), ()))
-    spectra = lax.dot_general(fwd[...], wave[...], nt, preferred_element_type=f32).astype(bf16)
+    samples = jnp.concatenate([wave[:, s, :] for s in range(SEGL)], axis=0)
+    spectra = lax.dot_general(fwd[...], samples, nt, preferred_element_type=f32).astype(bf16)
     values = spectra.astype(f32)
     squares = values * values
     sq_hi = squares.astype(bf16)
@@ -128,7 +141,6 @@
     for b in range(BAND):
         sb[b, :ROWS] = spectra[b * ROWS : (b + 1) * ROWS]
         sb[b, ROWS:] = energies
-    g[1088:, :] = jnp.zeros((JALL - 1088, WIDE), bf16)
     rb[0] = sb[band]
 
     pl.semaphore_wait(barrier, len(peers))
@@ -187,16 +199,19 @@
             for v in range(2):
                 g[pl.ds(own_row, CH), base + v * 128 : base + (v + 1) * 128] = halves[v].astype(bf16)
 
-    def slot(r, half=None):
-        if half is None:
-            return g.at[pl.ds(POS[r] * 64, 64)]
-        return g.at[pl.ds(pl.multiple_of(POS[r] * 64 + half * CH, CH), CH)]
+    def slot(r, half=None, instead=None, when=None):
+        row = POS[r] * 64
+        if half is not None:
+            return g.at[pl.ds(pl.multiple_of(row + half * CH, CH), CH)]
+        if instead is not None:
+            row = pl.multiple_of(row + when * (POS[instead] - POS[r]) * 64, 64)
+        return g.at[pl.ds(row, 64)]
 
     copies = {}
 
-    def move(name, src, dst, to):
+    def describe(name, src, dst, to):
         n = len(copies)
-        copy = pltpu.make_async_remote_copy(
+        copies[name] = pltpu.make_async_remote_copy(
             src_ref=src,
             dst_ref=dst,
             send_sem=g_send.at[n],
@@ -204,12 +219,60 @@
             device_id=at_tile(to),
             device_id_type=MESH,
         )
-        copy.start()
-        copies[name] = copy
-
-    move("z", slot(0, z), slot(0, z), other_z)
-    move("x1", slot(0, z), slot(8, z), tile + 16)
-    move("x2", slot(0, z), slot(16, z), tile + 32)
+
+    describe("z", slot(0, z), slot(0, z), other_z)
+    for name, half in (("", z), ("s", 1 - z)):
+        describe("x1" + name, slot(0, half), slot(8, half), tile + 16)
+        describe("x2" + name, slot(0, half), slot(16, half), tile + 32)
+    for k in range(1, 5):
+        describe(k, slot(k - 1, instead=7 + k, when=last), slot(k), above)
+        if k < 4:
+            describe(8 - k, slot(9 - k), slot(8 - k), tile - 2)
+        if 1 < k < 4:
+            describe(8 + k, slot(7 + k), slot(8 + k), tile + 2)
+        if k > 1:
+            describe(16 - k, slot(17 - k, instead=9 - k, when=first), slot(16 - k), below)
+    describe(9, slot(1), slot(9), tile + 16)
+    describe(15, slot(7), slot(15), tile + 16)
+
+    def start(name):
+        copies[name].start()
+
+    def arrive(r):
+        if r == 0:
+            copies["z"].wait_recv()
+            start("x1s")
+            start("x2s")
+            pl.when(last == 0)(lambda: start(1))
+        elif r in (8, 16):
+            name = {8: "x1", 16: "x2"}[r]
+            copies[name].wait_recv()
+            copies[name + "s"].wait_recv()
+            if r == 8:
+                pl.when(last == 1)(lambda: start(1))
+                start(7)
+        else:
+            copies[r].wait_recv()
+            if r < 4:
+                pl.when(last == 0)(lambda: start(r + 1))
+                if r == 1:
+                    start(9)
+            elif 4 < r < 8:
+                if r == 7:
+                    start(15)
+                if r > 5:
+                    start(r - 1)
+                pl.when(first == 1)(lambda: start(r + 7))
+            elif 8 < r < 12:
+                pl.when(last == 1)(lambda: start(r - 7))
+                if r < 11:
+                    start(r + 1)
+            elif r > 12:
+                pl.when(first == 0)(lambda: start(r - 1))
+
+    start("z")
+    start("x1")
+    start("x2")
 
     even = lax.rem(lane, 2) == 0
     bin4 = lax.rem(lane // 2, 4)
@@ -224,48 +287,19 @@
                         row = h * 128 + q * 32 + p * 16
                         wt[n, row : row + 16, v * 128 : (v + 1) * 128] = kept[h * 16 : h * 16 + 16]
 
-    def forward(kind, k):
-        if kind == "fa":
-            src, dst, to = k - 1, k, tile + 2
-        elif kind == "fb":
-            src, dst, to = 8 + k - 1, 8 + k, tile + 2
-        elif kind == "ba":
-            src, dst, to = 8 - (k - 1), 8 - k, tile - 2
-        else:
-            src, dst, to = 16 - (k - 1), 16 - k, tile - 2
-        move(kind + str(k), slot(src), slot(dst), to)
-
-    def arrive(kind, k, last):
-        copies[kind + str(k)].wait_recv()
-        if k < last:
-            forward(kind, k + 1)
-
-    copies["z"].wait_recv()
-    move("x1s", slot(0, 1 - z), slot(8, 1 - z), tile + 16)
-    move("x2s", slot(0, 1 - z), slot(16, 1 - z), tile + 32)
-    forward("fa", 1)
-    copies["x1"].wait_recv()
-    copies["x1s"].wait_recv()
-    forward("ba", 1)
-    forward("fb", 1)
-    copies["x2"].wait_recv()
-    copies["x2s"].wait_recv()
-    forward("bb", 1)
-
     def compute(k):
-        start, size = CHUNKS[k]
-        mine = bufs[k][0]
         for n in range(GROUPS):
-            block = g[start : start + size, n * 256 : (n + 1) * 256]
+            block = g[k * 128 : (k + 1) * 128, n * 256 : (n + 1) * 256]
             cross = lax.dot_general(wt[n], block, nt, preferred_element_type=f32).astype(bf16)
             for h in range(2):
-                ct[h, n * 128 : (n + 1) * 128, :size] = cross[h * 128 : (h + 1) * 128]
+                ct[n * 128 : (n + 1) * 128, h * 128 : (h + 1) * 128] = cross[h * 128 : (h + 1) * 128]
+        lags = jnp.dot(kt[...], ct[...], preferred_element_type=f32) * SCALE
         for h in range(2):
-            lags = jnp.dot(kt[...], ct[h, :, :size], preferred_element_type=f32) * SCALE
             for b4 in range(4):
-                mine[b4 % 2, 2 * h + b4 // 2] = lags[b4 * PART : (b4 + 1) * PART].astype(bf16)
-
-    sums = {}
+                share = lags[b4 * PART : (b4 + 1) * PART, h * 128 : (h + 1) * 128]
+                parts[k, b4 % 2, 2 * h + b4 // 2] = share.astype(bf16)
+
+    adding = {}
 
     def send(name, n, k, src, dst, to):
         copy = pltpu.make_async_remote_copy(
@@ -277,82 +311,60 @@
             device_id_type=MESH,
         )
         copy.start()
-        sums[(name, k)] = copy
+        adding[(name, k)] = copy
 
     up, down, far = lax.rem(zh + 1, 4), lax.rem(zh + 3, 4), lax.rem(zh + 2, 4)
     to_sibling, to_up, to_down = 2 * zh + 1 - core, 2 * up + core, 2 * down + core
 
     def r0(k):
         compute(k)
-        send("sib", 0, k, bufs[k][0].at[1 - core], bufs[k][1], to_sibling)
+        send("sib", 0, k, parts.at[k, 1 - core], theirs.at[k], to_sibling)
 
     def r1(k):
-        mine, theirs, both, h1, h2, _ = bufs[k]
-        sums[("sib", k)].wait_recv()
+        adding[("sib", k)].wait_recv()
         for n in (far, up, down, zh):
-            both[n] = (mine[core, n].astype(f32) + theirs[n].astype(f32)).astype(bf16)
+            both = parts[k, core, n].astype(f32) + theirs[k, n].astype(f32)
+            sums[k, n] = both.astype(bf16)
             if n is far:
-                send("ha", 1, k, both.at[far, pl.ds(0, HALF_A)], h1, to_up)
-                send("hb", 2, k, both.at[far, pl.ds(HALF_A, PART - HALF_A)], h2, to_down)
+                send("ha", 1, k, sums.at[k, far, pl.ds(0, HALF_A)], h1.at[k], to_up)
+                send("hb", 2, k, sums.at[k, far, pl.ds(HALF_A, PART - HALF_A)], h2.at[k], to_down)
 
     def r2(k):
-        _, _, both, h1, h2, final = bufs[k]
-        sums[("ha", k)].wait_recv()
-        both[up, :HALF_A] = (both[up, :HALF_A].astype(f32) + h1[...].astype(f32)).astype(bf16)
-        send("fu", 3, k, both.at[up], final.at[0], to_up)
-        sums[("hb", k)].wait_recv()
-        both[down, HALF_A:] = (both[down, HALF_A:].astype(f32) + h2[...].astype(f32)).astype(bf16)
-        send("fd", 4, k, both.at[down], final.at[1], to_down)
+        adding[("ha", k)].wait_recv()
+        both = sums[k, up, :HALF_A].astype(f32) + h1[k].astype(f32)
+        sums[k, up, :HALF_A] = both.astype(bf16)
+        send("fu", 3, k, sums.at[k, up], final.at[k, 0], to_up)
+        adding[("hb", k)].wait_recv()
+        both = sums[k, down, HALF_A:].astype(f32) + h2[k].astype(f32)
+        sums[k, down, HALF_A:] = both.astype(bf16)
+        send("fd", 4, k, sums.at[k, down], final.at[k, 1], to_down)
 
     def r3(k):
-        _, _, both, _, _, final = bufs[k]
-        start, size = CHUNKS[k]
-        sums[("fu", k)].wait_recv()
-        sums[("fd", k)].wait_recv()
-        whole = both[zh].astype(f32) + final[0].astype(f32) + final[1].astype(f32)
-        out[:, start : start + size] = whole.astype(bf16)
+        adding[("fu", k)].wait_recv()
+        adding[("fd", k)].wait_recv()
+        whole = sums[k, zh].astype(f32) + final[k, 0].astype(f32) + final[k, 1].astype(f32)
+        out[:, k * 128 : (k + 1) * 128] = whole.astype(bf16)
 
     kt_copy.wait()
-    arrive("fa", 1, 4)
-    arrive("ba", 1, 3)
-    r0(0)
-    arrive("fb", 1, 3)
-    arrive("bb", 1, 4)
-    r1(0)
-    arrive("fa", 2, 4)
-    arrive("ba", 2, 3)
-    r0(1)
-    r2(0)
-    arrive("fb", 2, 3)
-    arrive("bb", 2, 4)
-    r1(1)
-    arrive("fa", 3, 4)
-    arrive("ba", 3, 3)
-    r0(2)
-    r2(1)
-    r3(0)
-    arrive("fb", 3, 3)
-    arrive("bb", 3, 4)
-    r1(2)
-    arrive("fa", 4, 4)
-    arrive("bb", 4, 4)
-    r0(3)
-    r2(2)
-    r1(3)
-    r0(4)
-    r3(1)
-    r2(3)
-    r1(4)
-    r3(2)
-    r2(4)
-    r3(3)
-    r3(4)
+    for k in range(CHUNKS):
+        for r in ORDER[2 * k : 2 * k + 2]:
+            arrive(r)
+        r0(k)
+        if k >= 2:
+            r2(k - 2)
+        if k >= 4:
+            r3(k - 4)
+        r1(k)
+    r2(CHUNKS - 2)
+    r2(CHUNKS - 1)
+    for k in range(CHUNKS - 4, CHUNKS):
+        r3(k)
 
     for copy in exchange:
         copy.wait_send()
     for copy in copies.values():
         copy.wait_send()
-    for copy in sums.values():
+    for copy in adding.values():
         copy.wait_send()
 
 
@@ -376,49 +388,47 @@
 
 def body(waveforms, band_widths, pair_table):
     slots = pair_table.shape[1]
-    wave = jnp.transpose(waveforms, (1, 0, 2)).reshape(SEGL * CH, SAMPLES)
-    wave = jnp.pad(wave, ((0, 0), (0, 512 - SAMPLES)))
     bf16 = jnp.bfloat16
     scratch = [
+        pltpu.SMEM((BAND,), jnp.int32),
+        pltpu.VMEM(waveforms.shape, bf16),
+        pltpu.VMEM((BAND * ROWS, SAMPLES), bf16),
         pltpu.VMEM((BAND, 64, 128), bf16),
         pltpu.VMEM((BAND, 64, 128), bf16),
         pltpu.VMEM((JALL, WIDE), bf16),
         pltpu.VMEM((GROUPS, 256, 256), bf16),
         pltpu.VMEM((4 * PART, GROUPS * 128), bf16),
-        pltpu.VMEM((2, GROUPS * 128, 256), bf16),
+        pltpu.VMEM((GROUPS * 128, 256), bf16),
+        pltpu.VMEM((CHUNKS, 2, 4, PART, 128), bf16),
+        pltpu.VMEM((CHUNKS, 4, PART, 128), bf16),
+        pltpu.VMEM((CHUNKS, 4, PART, 128), bf16),
+        pltpu.VMEM((CHUNKS, HALF_A, 128), bf16),
+        pltpu.VMEM((CHUNKS, PART - HALF_A, 128), bf16),
+        pltpu.VMEM((CHUNKS, 2, PART, 128), bf16),
     ]
-    for _, size in CHUNKS:
-        scratch += [
-            pltpu.VMEM((2, 4, PART, size), bf16),
-            pltpu.VMEM((4, PART, size), bf16),
-            pltpu.VMEM((4, PART, size), bf16),
-            pltpu.VMEM((HALF_A, size), bf16),
-            pltpu.VMEM((PART - HALF_A, size), bf16),
-            pltpu.VMEM((2, PART, size), bf16),
-        ]
     dma = pltpu.SemaphoreType.DMA
     scratch += [
-        dma,
+        dma((4,)),
         dma((BAND,)),
         dma((BAND,)),
         dma((19,)),
         dma((19,)),
-        dma((5 * len(CHUNKS),)),
-        dma((5 * len(CHUNKS),)),
+        dma((5 * CHUNKS,)),
+        dma((5 * CHUNKS,)),
     ]
     vmem = pl.BlockSpec(memory_space=pltpu.VMEM)
     smem = pl.BlockSpec(memory_space=pltpu.SMEM)
     summed = pl.pallas_call(
         _main_kernel,
         out_shape=jax.ShapeDtypeStruct((PART, JALL), bf16),
-        in_specs=[smem, vmem, vmem, pl.BlockSpec(memory_space=pl.ANY)],
+        in_specs=[pl.BlockSpec(memory_space=pl.ANY)] * 4,
         out_specs=vmem,
         scratch_shapes=scratch,
         compiler_params=pltpu.CompilerParams(
-            collective_id=0, has_side_effects=True, vmem_limit_bytes=40 * 1024 * 1024
+            collective_id=0, has_side_effects=True, vmem_limit_bytes=60 * 1024 * 1024
         ),
         name="correlate",
-    )(band_widths, wave, jnp.asarray(_forward_const()), jnp.asarray(_inverse_const()))
+    )(band_widths, waveforms, jnp.asarray(_forward_const()), jnp.asarray(_inverse_const()))
     place = np.zeros((TILE // 2,), np.int32)
     for r, i in POS.items():
         place[r] = i

time: 111 us -> 90.2 us (0.81)
  the two profiles are of different devices: /device:TPU:68 before, /device:TPU:1 now
where the time goes in v2:
time: 90.2 us; the launch traced here: 90 us
  Pallas kernels  88.9 us (99%)
  local copies, waits for them, and re-layouts  1.03 us (1%)
    pallas_call x1, Pallas kernels, body(): pl.pallas_call(_main_kernel, out_shape=jax.ShapeDtypeStruct((PART, JALL),...  85.9 us
    pallas_call x1, Pallas kernels, body(): pl.pallas_call(_place_kernel, out_shape=jax.ShapeDtypeStruct((slots, 4, C...  2.98 us

profile of v2, /device:TPU:1, one launch (start us, length us, event | category | flops | bytes accessed | tf_op | source)
XLA Modules:
  0.0 90.0 jit_solution(4032552585425436393)
XLA Ops:
  0.0 0.0 copy-start.1
  0.0 0.0 copy-start.3
  0.0 0.0 copy-start.2
  0.0 85.9 %correlate.1.summed = bf16[208,1152]{1,0:T(8,128)(2,1)} custom-call(s32[8]{0:T(128)} %widths_hbm.1, bf16[32,4,500]{2,1,0:T(4,128)(2,1)} %wave_hbm.1, bf16[384,500]{1,0:T(8,128)(2,1)} %constant.8.clone.fwd_hbm, bf16[8,832,768]{2,1,0:T(8,128)(2,1)} %constant.9.clone.inv_all), custom_call_target="tpu_custom_call" | custom-call | tf_op jit(solution)/shard_map/correlate/pallas_call | solution.py:421
  86.0 0.0 copy-done.1
  86.0 0.0 copy-done.3
  86.0 0.0 copy-done.2
  86.0 0.0 copy-start
  86.0 1.0 %copy-done = bf16[208,1152]{1,0:T(8,128)(2,1)S(1)} copy-done((bf16[208,1152]{1,0:T(8,128)(2,1)S(1)}, bf16[208,1152]{1,0:T(8,128)(2,1)}, u32[]{:S(2)}) %copy-start) | copy-done | bytes 479256
  87.0 3.0 %place.2 = bf16[33,4,32,51]{3,2,1,0:T(8,128)(2,1)} custom-call(s32[1,33]{1,0:T(1,128)S(1)} %copy-done.2, s32[32]{0:T(128)S(1)} %copy-done.3, bf16[208,1152]{1,0:T(8,128)(2,1)S(1)} %copy-done, bf16[208,512]{1,0:T(8,128)(2,1)S(1)} %copy-done.1), custom_call_target="tpu_custom_call" | custom-call | tf_op jit(solution)/shard_map/place/pallas_call | solution.py:435
Async XLA Ops:
  0.0 86.0 %copy-start.1 = (bf16[208,512]{1,0:T(8,128)(2,1)S(1)}, bf16[208,512]{1,0:T(8,128)(2,1)}, u32[]{:S(2)}) copy-start(bf16[208,512]{1,0:T(8,128)(2,1)} %constant.11.clone.select) | copy-start | bytes 638980
  0.0 86.0 %copy-start.3 = (s32[32]{0:T(128)S(1)}, s32[32]{0:T(128)}, u32[]{:S(2)}) copy-start(s32[32]{0:T(128)} %constant.10.clone.place) | copy-start | bytes 388
  0.0 86.0 %copy-start.2 = (s32[1,33]{1,0:T(1,128)S(1)}, s32[1,33]{1,0:T(1,128)}, u32[]{:S(2)}) copy-start(s32[1,33]{1,0:T(1,128)} %table.1) | copy-start | bytes 400
  86.0 1.0 %copy-start = (bf16[208,1152]{1,0:T(8,128)(2,1)S(1)}, bf16[208,1152]{1,0:T(8,128)(2,1)}, u32[]{:S(2)}) copy-start(bf16[208,1152]{1,0:T(8,128)(2,1)} %correlate.1.summed) | copy-start | bytes 1437700

commit v3 on v2

v3 whole, which is shorter than its diff:
```python
import functools
import math

import jax
import jax.numpy as jnp
import ml_dtypes
import numpy as np
from jax import lax
from jax.experimental import pallas as pl
from jax.experimental.pallas import tpu as pltpu
from jax.sharding import PartitionSpec as P

BINS = 180
FIRST = 20
LAGS = 51
SAMPLES = 500
EPS = 1e-05

BAND = 8
TILE = 64
CH = 32
SEG = 32
SEGL = 4
QN = 48
BINGROUPS = 4
GROUPS = QN // 4
ROWS = 2 * QN
MSG = ROWS + 16
WIDE = QN * 64
PART = 208
SCALE = 1.0 / math.sqrt(SEG * BINS)
MESH = pl.DeviceIdType.MESH

ORDER = [0, 8, 16, 1, 7, 9, 15, 2, 6, 10, 14, 3, 5, 11, 13, 4, 12]
POS = {r: i for i, r in enumerate(ORDER)}
CHUNKS = [(0, 4), (4, 4), (8, 4), (12, 2), (14, 2), (16, 1)]
PACKED = {4: PART, 2: 112, 1: 64}
REGION = 640
JALL = 2 * REGION
STEPS = [
    "8a", "1a", "1b", "8b", "16b", "16a", "7a", "9a", "9b", "7b", "c0",
    "2a", "15a", "s0", "2b", "15b", "10a", "10b", "6a", "c1",
    "3a", "s1", "6b", "14a", "3b", "14b", "c2",
    "5a", "m0", "11b", "11a", "5b", "s2", "c3",
    "13a", "4a", "m1", "s3", "4b", "13b", "c4",
    "s4", "12a", "m2", "12b", "c5",
    "s5", "m3", "m4", "m5", "f0", "f1", "f2", "f3", "f4", "f5",
]


def _forward_const():
    n = np.arange(SAMPLES)
    table = np.zeros((BINGROUPS * QN, 2, SAMPLES), np.float32)
    for k in range(BINS):
        angle = ((n * (FIRST + k)) % SAMPLES) * (2.0 * math.pi / SAMPLES)
        table[k, 0] = np.cos(angle)
        table[k, 1] = -np.sin(angle)
    return table.reshape(BINGROUPS * ROWS, SAMPLES).astype(ml_dtypes.bfloat16)


def _inverse_const():
    tau = np.arange(LAGS) - LAGS // 2
    table = np.zeros((BINGROUPS * QN, 2, LAGS), np.float32)
    for k in range(BINS):
        angle = (((FIRST + k) * tau) % SAMPLES) * (2.0 * math.pi / SAMPLES)
        table[k, 0] = np.cos(angle)
        table[k, 1] = -np.sin(angle)
    table = table.reshape(BINGROUPS, GROUPS, 4, 2, LAGS)
    out = np.zeros((BINGROUPS, 4, PART, GROUPS, 4, 2, 16), np.float32)
    for b4 in range(4):
        for i4 in range(4):
            rows = np.moveaxis(table, -1, 1)
            out[:, b4, i4 * LAGS : (i4 + 1) * LAGS, :, :, :, b4 * 4 + i4] = rows
    return out.reshape(BINGROUPS, 4 * PART, GROUPS * 128).astype(ml_dtypes.bfloat16)


def _select_const():
    out = np.zeros((PART, 512), np.float32)
    for i4 in range(4):
        for lag in range(LAGS):
            out[i4 * LAGS + lag, i4 * 128 + lag] = 1.0
    return out.astype(ml_dtypes.bfloat16)


def _main_kernel(widths_hbm, wave_hbm, fwd_hbm, inv_all, out, *scratch):
    widths, wave, fwd, sb, rb, g, wt, kt, ct = scratch[:9]
    parts, theirs, mine, pair_out, pair_in, outer, final = scratch[9:16]
    (in_sem, a_send, a_recv, o_send, o_recv, g_send, g_recv, r_send, r_recv) = scratch[16:]
    f32, bf16 = jnp.float32, jnp.bfloat16

    band = lax.axis_index("band")
    tile = lax.axis_index("tile")
    core = lax.rem(band, 2)
    zh = band // 2
    z = lax.rem(tile, 2)
    side = band // 4
    group = lax.rem(band, BINGROUPS)
    home = z == side
    y = lax.rem(tile // 2, 8)
    first = (7 - y) // 7
    last = (y + 1) // 8

    def at_band(b):
        return {"band": b, "tile": tile}

    def at_tile(t):
        return {"band": band, "tile": lax.rem(t + TILE, TILE)}

    barrier = pltpu.get_barrier_semaphore()
    peers = [at_band(lax.rem(band + o, BAND)) for o in range(1, BAND)]
    other_z = tile + 1 - 2 * z
    above, below = tile + 2 - 16 * last, tile - 2 + 16 * first
    peers += [at_tile(t) for t in (tile + 16, tile - 16, tile + 32)]
    peers += [at_tile(t) for t in (tile + 2, tile - 2, above, below)]
    for peer in peers:
        pl.semaphore_signal(barrier, inc=1, device_id=peer, device_id_type=MESH)

    @pl.when(jnp.logical_not(home))
    def _():
        for b in range(BAND):
            peer = {"band": b, "tile": other_z}
            pl.semaphore_signal(barrier, inc=1, device_id=peer, device_id_type=MESH)

    wave_copy = pltpu.make_async_copy(wave_hbm, wave, in_sem.at[0])
    fwd_copy = pltpu.make_async_copy(fwd_hbm, fwd, in_sem.at[1])
    widths_copy = pltpu.make_async_copy(widths_hbm, widths, in_sem.at[2])
    kt_copy = pltpu.make_async_copy(inv_all.at[group], kt, in_sem.at[3])
    for copy in (wave_copy, fwd_copy, widths_copy, kt_copy):
        copy.start()
    wave_copy.wait()
    fwd_copy.wait()
    widths_copy.wait()

    nt = (((1,), (1,)), ((), ()))
    samples = jnp.concatenate([wave[:, s, :] for s in range(SEGL)], axis=0)
    spectra = lax.dot_general(fwd[...], samples, nt, preferred_element_type=f32).astype(bf16)
    values = spectra.astype(f32)
    squares = values * values
    sq_hi = squares.astype(bf16)
    sq_lo = (squares - sq_hi.astype(f32)).astype(bf16)
    offsets = []
    total = widths[0] * 0
    for b in range(BAND):
        offsets.append(total)
        total = total + widths[b]

    def member(rows, bins):
        low = jnp.zeros(rows.shape, jnp.int32)
        size = jnp.zeros(rows.shape, jnp.int32)
        for b in range(BAND):
            low = jnp.where(rows == b, offsets[b], low)
            size = jnp.where(rows == b, widths[b], size)
        return jnp.where((bins >= low) & (bins < low + size), 1.0, 0.0).astype(f32)

    shape = (BAND, BINGROUPS * ROWS)
    is_in = member(
        lax.broadcasted_iota(jnp.int32, shape, 0), lax.broadcasted_iota(jnp.int32, shape, 1) // 2
    ).astype(bf16)
    part = jnp.dot(is_in, sq_hi, preferred_element_type=f32)
    part = part + jnp.dot(is_in, sq_lo, preferred_element_type=f32)
    part_hi = part.astype(bf16).astype(f32)
    energies = jnp.concatenate([part_hi, part - part_hi], axis=0).astype(bf16)
    for b in range(BINGROUPS):
        sb[b, :ROWS] = spectra[b * ROWS : (b + 1) * ROWS]
        sb[b, ROWS:] = energies
    rb[0, 0] = sb[group]

    pl.semaphore_wait(barrier, len(peers) + BINGROUPS)

    exchange = []
    for o in range(1, BAND):
        to = lax.rem(band + o, BAND)
        copy = pltpu.make_async_remote_copy(
            src_ref=sb.at[lax.rem(to, BINGROUPS)],
            dst_ref=rb.at[0, o],
            send_sem=a_send.at[o],
            recv_sem=a_recv.at[o],
            device_id=at_band(to),
            device_id_type=MESH,
        )
        copy.start()
        exchange.append(copy)
    across = []
    for j in range(BINGROUPS):
        to = 4 * z + j
        o = lax.rem(to - band + BAND, BAND)
        copy = pltpu.make_async_remote_copy(
            src_ref=sb.at[j],
            dst_ref=rb.at[1, o],
            send_sem=o_send.at[j],
            recv_sem=o_recv.at[o],
            device_id={"band": to, "tile": other_z},
            device_id_type=MESH,
        )
        copy.start()
        across.append(copy)

    lane = lax.broadcasted_iota(jnp.int32, (CH, 128), 1)

    def whiten(which):
        energy = jnp.zeros((BAND, 128), f32)
        for o in range(BAND):
            tail = rb[which, o, ROWS:].astype(f32)
            energy = energy + tail[:BAND] + tail[BAND:]
        energy = energy + pltpu.roll(energy, 64, 1)
        energy = energy + pltpu.roll(energy, 32, 1)
        row8 = lax.broadcasted_iota(jnp.int32, (BAND, 128), 0)
        width8 = jnp.ones((BAND, 128), f32)
        for b in range(BAND):
            width8 = jnp.where(row8 == b, widths[b].astype(f32), width8)
        gain = lax.rsqrt(energy / (SEG * width8) + EPS)
        bins = group * QN + lax.broadcasted_iota(jnp.int32, (ROWS, 128), 0) // 2
        gains = jnp.zeros((ROWS, 128), f32)
        for b in range(BAND):
            inside = (bins >= offsets[b]) & (bins < offsets[b] + widths[b])
            gains = jnp.where(inside, gain[b : b + 1, :], gains)
        white = [
            (rb[which, o, :ROWS].astype(f32) * gains).astype(bf16).astype(f32) for o in range(BAND)
        ]
        tiles = []
        for pair in range(GROUPS // 2):
            stack = jnp.concatenate(
                [
                    white[o][(2 * pair + h) * 8 : (2 * pair + h + 1) * 8]
                    for h in range(2)
                    for o in range(BAND)
                ],
                axis=0,
            )
            flipped = jnp.transpose(stack)
            rolled = pltpu.roll(flipped, 64, 1)
            seg = [flipped[s * CH : (s + 1) * CH] for s in range(SEGL)]
            seg_r = [rolled[s * CH : (s + 1) * CH] for s in range(SEGL)]
            for low, high in ((seg, seg_r), (seg_r, seg)):
                tiles.append([jnp.where(lane < 64, low[2 * v], high[2 * v + 1]) for v in range(2)])
        return tiles

    for copy in exchange:
        copy.wait_recv()

    @pl.when(jnp.logical_not(home))
    def _():
        for o in range(BAND):
            pltpu.make_async_remote_copy(
                src_ref=sb.at[0],
                dst_ref=rb.at[1, o],
                send_sem=o_send.at[0],
                recv_sem=o_recv.at[o],
                device_id={"band": band, "tile": other_z},
                device_id_type=MESH,
            ).wait_recv()

    for n, halves in enumerate(whiten(lax.rem(z + side, 2))):
        for v in range(2):
            g[:CH, n * 256 + v * 128 : n * 256 + (v + 1) * 128] = halves[v].astype(bf16)

    def slot(r, h, instead=None, when=None):
        row = POS[r] * CH
        if instead is not None:
            row = pl.multiple_of(row + when * (POS[instead] - POS[r]) * CH, CH)
        return g.at[pl.ds(row, CH), pl.ds(h * (WIDE // 2), WIDE // 2)]

    copies = {}

    def describe(name, src, dst, to):
        n = len(copies)
        copies[name] = pltpu.make_async_remote_copy(
            src_ref=src,
            dst_ref=dst,
            send_sem=g_send.at[n],
            recv_sem=g_recv.at[n],
            device_id=at_tile(to),
            device_id_type=MESH,
        )

    for h in range(2):
        describe((8, h), slot(0, h), slot(8, h), tile + 16)
        describe((16, h), slot(0, h), slot(16, h), tile + 32)
        for k in range(1, 5):
            describe((k, h), slot(k - 1, h, 7 + k, last), slot(k, h), above)
            if k < 4:
                describe((8 - k, h), slot(9 - k, h), slot(8 - k, h), tile - 2)
            if 1 < k < 4:
                describe((8 + k, h), slot(7 + k, h), slot(8 + k, h), tile + 2)
            if k > 1:
                describe((16 - k, h), slot(17 - k, h, 9 - k, first), slot(16 - k, h), below)
        describe((9, h), slot(1, h), slot(9, h), tile + 16)
        describe((15, h), slot(7, h), slot(15, h), tile + 16)

    def arrive(r, h):
        def start(other):
            copies[(other, h)].start()

        if r:
            copies[(r, h)].wait_recv()
        if r == 0:
            pl.when(last == 0)(lambda: start(1))
            start(8)
            start(16)
        elif r == 8:
            pl.when(last == 1)(lambda: start(1))
            start(7)
        elif r < 4:
            pl.when(last == 0)(lambda: start(r + 1))
            if r == 1:
                start(9)
        elif 4 < r < 8:
            if r > 5:
                start(r - 1)
            pl.when(first == 1)(lambda: start(r + 7))
            if r == 7:
                start(15)
        elif 8 < r < 12:
            pl.when(last == 1)(lambda: start(r - 7))
            if r < 11:
                start(r + 1)
        elif 12 < r < 16:
            pl.when(first == 0)(lambda: start(r - 1))

    arrive(0, 0)
    arrive(0, 1)

    even = lax.rem(lane, 2) == 0
    bin4 = lax.rem(lane // 2, 4)
    for n, halves in enumerate(whiten(0)):
        for v in range(2):
            own = halves[v]
            alt = jnp.where(even, pltpu.roll(own, 127, 1), -pltpu.roll(own, 1, 1))
            for q in range(4):
                for p in range(2):
                    kept = jnp.where(bin4 == q, own if p == 0 else alt, 0.0).astype(bf16)
                    for h in range(2):
                        row = h * 128 + q * 32 + p * 16
                        wt[n, row : row + 16, v * 128 : (v + 1) * 128] = kept[h * 16 : h * 16 + 16]

    wide = lax.broadcasted_iota(jnp.int32, (PART, 128), 1)

    def compute(k):
        start, blocks = CHUNKS[k]
        rows = PACKED[blocks]
        for n in range(GROUPS):
            block = g[start * CH : (start + blocks) * CH, n * 256 : (n + 1) * 256]
            block = jnp.concatenate([block] * (4 // blocks), axis=0)
            cross = lax.dot_general(wt[n], block, nt, preferred_element_type=f32).astype(bf16)
            for h in range(2):
                ct[n * 128 : (n + 1) * 128, h * 128 : (h + 1) * 128] = cross[h * 128 : (h + 1) * 128]
        lags = jnp.dot(kt[...], ct[...], preferred_element_type=f32) * SCALE
        for h in range(2):
            for b4 in range(4):
                share = lags[b4 * PART : (b4 + 1) * PART, h * 128 : (h + 1) * 128]
                if blocks < 4:
                    copies_of = 4 // blocks
                    step = (PART - rows) // (copies_of - 1)
                    packed = share[:rows]
                    for i in range(1, copies_of):
                        here = wide[:rows] // (32 * blocks) == i
                        packed = jnp.where(here, share[i * step : i * step + rows], packed)
                    share = packed
                parts[k, b4 % 2, 2 * h + b4 // 2, :rows] = share.astype(bf16)

    def place(k, region, share):
        start, blocks = CHUNKS[k]
        rows = PACKED[blocks]
        base = region * REGION + start * CH
        if blocks < 4:
            copies_of = 4 // blocks
            step = (PART - rows) // (copies_of - 1)
            pieces = [share]
            for i in range(1, copies_of):
                pieces.append(pltpu.roll(share, 128 - 32 * blocks * i, 1)[rows - step :])
            share = jnp.concatenate(pieces, axis=0)
            shift = base % 128
            if shift:
                share = pltpu.roll(share, shift, 1)
            out[:, base : base + 32 * blocks] = share[:, shift : shift + 32 * blocks].astype(bf16)
        else:
            out[:, base : base + 128] = share.astype(bf16)

    adding = {}

    def send(name, n, k, src, dst, to):
        copy = pltpu.make_async_remote_copy(
            src_ref=src,
            dst_ref=dst,
            send_sem=r_send.at[k * 3 + n],
            recv_sem=r_recv.at[k * 3 + n],
            device_id=at_band(to),
            device_id_type=MESH,
        )
        copy.start()
        adding[(name, k)] = copy

    odd = lax.rem(zh, 2)
    mate, beyond, far = zh + 1 - 2 * odd, lax.rem(zh + 2 * odd + 3, 4), lax.rem(zh + 2, 4)
    to_sibling, to_mate, to_beyond = 2 * zh + 1 - core, 2 * mate + core, 2 * beyond + core

    def r0(k):
        compute(k)
        rows = pl.ds(0, PACKED[CHUNKS[k][1]])
        send("sib", 0, k, parts.at[k, 1 - core, :, rows], theirs.at[k, :, rows], to_sibling)

    def r1(k):
        rows = PACKED[CHUNKS[k][1]]
        adding[("sib", k)].wait_recv()

        def both(n):
            return parts[k, core, n, :rows].astype(f32) + theirs[k, n, :rows].astype(f32)

        pair_out[k, 0, :rows] = both(mate).astype(bf16)
        pair_out[k, 1, :rows] = both(far).astype(bf16)
        cut = pl.ds(0, rows)
        send("pair", 1, k, pair_out.at[k, :, cut], pair_in.at[k, :, cut], to_mate)
        outer[k, :rows] = both(beyond).astype(bf16)
        mine[k, :rows] = both(zh).astype(bf16)

    def r2(k):
        rows = PACKED[CHUNKS[k][1]]
        adding[("pair", k)].wait_recv()
        outer[k, :rows] = (outer[k, :rows].astype(f32) + pair_in[k, 1, :rows].astype(f32)).astype(bf16)
        send("out", 2, k, outer.at[k, pl.ds(0, rows)], final.at[k, pl.ds(0, rows)], to_beyond)
        place(k, 0, mine[k, :rows].astype(f32) + pair_in[k, 0, :rows].astype(f32))

    def r3(k):
        rows = PACKED[CHUNKS[k][1]]
        adding[("out", k)].wait_recv()
        place(k, 1, final[k, :rows].astype(f32))

    kt_copy.wait()
    out[:, 17 * CH : REGION] = jnp.zeros((PART, REGION - 17 * CH), bf16)
    out[:, REGION + 17 * CH :] = jnp.zeros((PART, REGION - 17 * CH), bf16)
    stages = {"c": r0, "s": r1, "m": r2, "f": r3}
    for step in STEPS:
        if step[0] in stages:
            stages[step[0]](int(step[1:]))
        else:
            arrive(int(step[:-1]), "ab".index(step[-1]))

    for copy in exchange + across:
        copy.wait_send()
    for copy in copies.values():
        copy.wait_send()
    for copy in adding.values():
        copy.wait_send()


def _place_kernel(table, place, summed, select, out, turned):
    tile = lax.axis_index("tile")
    side = lax.axis_index("band") // 4
    rows = lax.dot_general(
        summed[...], select[...], (((0,), (0,)), ((), ())), preferred_element_type=jnp.float32
    )
    turned[...] = rows.astype(jnp.bfloat16).reshape(turned.shape)

    def step(s, carry):
        partner = table[0, s]
        behind = lax.rem(tile // 2 - partner // 2 + TILE // 2, TILE // 2)
        other = lax.rem(partner + side, 2)
        block = place[behind] + other * (REGION // CH)
        for i4 in range(4):
            out[s, i4] = turned[block, :, i4 * 128 : i4 * 128 + LAGS]
        return carry

    lax.fori_loop(0, out.shape[0], step, 0)


def body(waveforms, band_widths, pair_table):
    slots = pair_table.shape[1]
    bf16 = jnp.bfloat16
    scratch = [
        pltpu.SMEM((BAND,), jnp.int32),
        pltpu.VMEM(waveforms.shape, bf16),
        pltpu.VMEM((BINGROUPS * ROWS, SAMPLES), bf16),
        pltpu.VMEM((BINGROUPS, MSG, 128), bf16),
        pltpu.VMEM((2, BAND, MSG, 128), bf16),
        pltpu.VMEM((17 * CH, WIDE), bf16),
        pltpu.VMEM((GROUPS, 256, 256), bf16),
        pltpu.VMEM((4 * PART, GROUPS * 128), bf16),
        pltpu.VMEM((GROUPS * 128, 256), bf16),
        pltpu.VMEM((len(CHUNKS), 2, 4, PART, 128), bf16),
        pltpu.VMEM((len(CHUNKS), 4, PART, 128), bf16),
        pltpu.VMEM((len(CHUNKS), PART, 128), bf16),
        pltpu.VMEM((len(CHUNKS), 2, PART, 128), bf16),
        pltpu.VMEM((len(CHUNKS), 2, PART, 128), bf16),
        pltpu.VMEM((len(CHUNKS), PART, 128), bf16),
        pltpu.VMEM((len(CHUNKS), PART, 128), bf16),
    ]
    dma = pltpu.SemaphoreType.DMA
    scratch += [
        dma((4,)),
        dma((BAND,)),
        dma((BAND,)),
        dma((BINGROUPS,)),
        dma((BAND,)),
        dma((32,)),
        dma((32,)),
        dma((3 * len(CHUNKS),)),
        dma((3 * len(CHUNKS),)),
    ]
    vmem = pl.BlockSpec(memory_space=pltpu.VMEM)
    smem = pl.BlockSpec(memory_space=pltpu.SMEM)
    summed = pl.pallas_call(
        _main_kernel,
        out_shape=jax.ShapeDtypeStruct((PART, JALL), bf16),
        in_specs=[pl.BlockSpec(memory_space=pl.ANY)] * 4,
        out_specs=vmem,
        scratch_shapes=scratch,
        compiler_params=pltpu.CompilerParams(
            collective_id=0, has_side_effects=True, vmem_limit_bytes=60 * 1024 * 1024
        ),
        name="correlate",
    )(band_widths, waveforms, jnp.asarray(_forward_const()), jnp.asarray(_inverse_const()))
    place = np.zeros((TILE // 2,), np.int32)
    for r, i in POS.items():
        place[r] = i
    placed = pl.pallas_call(
        _place_kernel,
        out_shape=jax.ShapeDtypeStruct((slots, 4, CH, LAGS), bf16),
        in_specs=[smem, smem, vmem, vmem],
        out_specs=vmem,
        scratch_shapes=[pltpu.VMEM((JALL // CH, CH, 512), bf16)],
        compiler_params=pltpu.CompilerParams(vmem_limit_bytes=32 * 1024 * 1024),
        name="place",
    )(pair_table, jnp.asarray(place), summed, jnp.asarray(_select_const()))
    return placed[None]


def solution(mesh):
    placed = (P("tile", "band", None), P(), P("tile", None))
    return jax.shard_map(
        body,
        mesh=mesh,
        in_specs=placed,
        out_specs=P("tile", None, "band", None, None),
        check_vma=False,
    )
```

time: 90.2 us -> 83.6 us (0.927)
  Pallas kernels: 88.9 us -> 82 us
    pallas_call x1, Pallas kernels: 85.9 us -> 79 us  [body(): pl.pallas_call(_main_kernel, out_shape=jax.ShapeDtypeStruct((PART, JALL),...]
where the time goes in v3:
time: 83.6 us; the launch traced here: 83.1 us
  Pallas kernels  82 us (98%)
  local copies, waits for them, and re-layouts  1.05 us (1%)
    pallas_call x1, Pallas kernels, body(): pl.pallas_call(_main_kernel, out_shape=jax.ShapeDtypeStruct((PART, JALL),...  79 us
    pallas_call x1, Pallas kernels, body(): pl.pallas_call(_place_kernel, out_shape=jax.ShapeDtypeStruct((slots, 4, C...  3.01 us

profile of v3, /device:TPU:1, one launch (start us, length us, event | category | flops | bytes accessed | tf_op | source)
XLA Modules:
  0.0 83.1 jit_solution(10493778536215550816)
XLA Ops:
  0.0 0.0 copy-start.1
  0.0 0.0 copy-start.3
  0.0 0.0 copy-start.2
  0.0 79.0 %correlate.1.summed = bf16[208,1280]{1,0:T(8,128)(2,1)} custom-call(s32[8]{0:T(128)} %widths_hbm.1, bf16[32,4,500]{2,1,0:T(4,128)(2,1)} %wave_hbm.1, bf16[384,500]{1,0:T(8,128)(2,1)} %constant.8.clone.fwd_hbm, bf16[4,832,1536]{2,1,0:T(8,128)(2,1)} %constant.9.clone.inv_all), custom_call_target="tpu_custom_call" | custom-call | tf_op jit(solution)/shard_map/correlate/pallas_call | solution.py:501
  79.1 0.0 copy-done.1
  79.1 0.0 copy-done.3
  79.1 0.0 copy-done.2
  79.1 0.0 copy-start
  79.1 1.0 %copy-done = bf16[208,1280]{1,0:T(8,128)(2,1)S(1)} copy-done((bf16[208,1280]{1,0:T(8,128)(2,1)S(1)}, bf16[208,1280]{1,0:T(8,128)(2,1)}, u32[]{:S(2)}) %copy-start) | copy-done | bytes 532504
  80.1 3.0 %place.2 = bf16[33,4,32,51]{3,2,1,0:T(8,128)(2,1)} custom-call(s32[1,33]{1,0:T(1,128)S(1)} %copy-done.2, s32[32]{0:T(128)S(1)} %copy-done.3, bf16[208,1280]{1,0:T(8,128)(2,1)S(1)} %copy-done, bf16[208,512]{1,0:T(8,128)(2,1)S(1)} %copy-done.1), custom_call_target="tpu_custom_call" | custom-call | tf_op jit(solution)/shard_map/place/pallas_call | solution.py:515
Async XLA Ops:
  0.0 79.1 %copy-start.1 = (bf16[208,512]{1,0:T(8,128)(2,1)S(1)}, bf16[208,512]{1,0:T(8,128)(2,1)}, u32[]{:S(2)}) copy-start(bf16[208,512]{1,0:T(8,128)(2,1)} %constant.11.clone.select) | copy-start | bytes 638980
  0.0 79.1 %copy-start.3 = (s32[32]{0:T(128)S(1)}, s32[32]{0:T(128)}, u32[]{:S(2)}) copy-start(s32[32]{0:T(128)} %constant.10.clone.place) | copy-start | bytes 388
  0.0 79.1 %copy-start.2 = (s32[1,33]{1,0:T(1,128)S(1)}, s32[1,33]{1,0:T(1,128)}, u32[]{:S(2)}) copy-start(s32[1,33]{1,0:T(1,128)} %table.1) | copy-start | bytes 400
  79.1 1.0 %copy-start = (bf16[208,1280]{1,0:T(8,128)(2,1)S(1)}, bf16[208,1280]{1,0:T(8,128)(2,1)}, u32[]{:S(2)}) copy-start(bf16[208,1280]{1,0:T(8,128)(2,1)} %correlate.1.summed) | copy-start | bytes 1597444

commit v4 on v3

--- a/solution.py
+++ b/solution.py
@@ -35,16 +35,15 @@
 POS = {r: i for i, r in enumerate(ORDER)}
 CHUNKS = [(0, 4), (4, 4), (8, 4), (12, 2), (14, 2), (16, 1)]
 PACKED = {4: PART, 2: 112, 1: 64}
-REGION = 640
-JALL = 2 * REGION
+DIRECT = (4, 5)
 STEPS = [
-    "8a", "1a", "1b", "8b", "16b", "16a", "7a", "9a", "9b", "7b", "c0",
+    "1b", "7a", "9a", "16a", "16b", "7b", "9b", "c0",
     "2a", "15a", "s0", "2b", "15b", "10a", "10b", "6a", "c1",
     "3a", "s1", "6b", "14a", "3b", "14b", "c2",
     "5a", "m0", "11b", "11a", "5b", "s2", "c3",
     "13a", "4a", "m1", "s3", "4b", "13b", "c4",
     "s4", "12a", "m2", "12b", "c5",
-    "s5", "m3", "m4", "m5", "f0", "f1", "f2", "f3", "f4", "f5",
+    "m3", "s5", "f0", "f1", "f2", "f3", "m4", "f4", "m5", "f5",
 ]
 
 
@@ -82,10 +81,10 @@
     return out.astype(ml_dtypes.bfloat16)
 
 
-def _main_kernel(widths_hbm, wave_hbm, fwd_hbm, inv_all, out, *scratch):
+def _main_kernel(widths_hbm, wave_hbm, fwd_hbm, inv_all, select_hbm, out, *scratch):
     widths, wave, fwd, sb, rb, g, wt, kt, ct = scratch[:9]
-    parts, theirs, mine, pair_out, pair_in, outer, final = scratch[9:16]
-    (in_sem, a_send, a_recv, o_send, o_recv, g_send, g_recv, r_send, r_recv) = scratch[16:]
+    parts, theirs, mine, pair_out, pair_in, outer, final, select = scratch[9:17]
+    (in_sem, a_send, a_recv, o_send, o_recv, g_send, g_recv, r_send, r_recv) = scratch[17:]
     f32, bf16 = jnp.float32, jnp.bfloat16
 
     band = lax.axis_index("band")
@@ -125,7 +124,8 @@
     fwd_copy = pltpu.make_async_copy(fwd_hbm, fwd, in_sem.at[1])
     widths_copy = pltpu.make_async_copy(widths_hbm, widths, in_sem.at[2])
     kt_copy = pltpu.make_async_copy(inv_all.at[group], kt, in_sem.at[3])
-    for copy in (wave_copy, fwd_copy, widths_copy, kt_copy):
+    select_copy = pltpu.make_async_copy(select_hbm, select, in_sem.at[4])
+    for copy in (wave_copy, fwd_copy, widths_copy, kt_copy, select_copy):
         copy.start()
     wave_copy.wait()
     fwd_copy.wait()
@@ -252,13 +252,14 @@
 
     for n, halves in enumerate(whiten(lax.rem(z + side, 2))):
         for v in range(2):
-            g[:CH, n * 256 + v * 128 : n * 256 + (v + 1) * 128] = halves[v].astype(bf16)
+            first_lane = n % (GROUPS // 2) * 256 + v * 128
+            g[n // (GROUPS // 2), :CH, first_lane : first_lane + 128] = halves[v].astype(bf16)
 
     def slot(r, h, instead=None, when=None):
         row = POS[r] * CH
         if instead is not None:
             row = pl.multiple_of(row + when * (POS[instead] - POS[r]) * CH, CH)
-        return g.at[pl.ds(row, CH), pl.ds(h * (WIDE // 2), WIDE // 2)]
+        return g.at[h, pl.ds(row, CH)]
 
     copies = {}
 
@@ -296,7 +297,6 @@
         if r == 0:
             pl.when(last == 0)(lambda: start(1))
             start(8)
-            start(16)
         elif r == 8:
             pl.when(last == 1)(lambda: start(1))
             start(7)
@@ -319,6 +319,8 @@
 
     arrive(0, 0)
     arrive(0, 1)
+    for h in range(2):
+        copies[(16, h)].start()
 
     even = lax.rem(lane, 2) == 0
     bin4 = lax.rem(lane // 2, 4)
@@ -339,7 +341,8 @@
         start, blocks = CHUNKS[k]
         rows = PACKED[blocks]
         for n in range(GROUPS):
-            block = g[start * CH : (start + blocks) * CH, n * 256 : (n + 1) * 256]
+            low = n % (GROUPS // 2) * 256
+            block = g[n // (GROUPS // 2), start * CH : (start + blocks) * CH, low : low + 256]
             block = jnp.concatenate([block] * (4 // blocks), axis=0)
             cross = lax.dot_general(wt[n], block, nt, preferred_element_type=f32).astype(bf16)
             for h in range(2):
@@ -361,7 +364,6 @@
     def place(k, region, share):
         start, blocks = CHUNKS[k]
         rows = PACKED[blocks]
-        base = region * REGION + start * CH
         if blocks < 4:
             copies_of = 4 // blocks
             step = (PART - rows) // (copies_of - 1)
@@ -369,12 +371,13 @@
             for i in range(1, copies_of):
                 pieces.append(pltpu.roll(share, 128 - 32 * blocks * i, 1)[rows - step :])
             share = jnp.concatenate(pieces, axis=0)
-            shift = base % 128
-            if shift:
-                share = pltpu.roll(share, shift, 1)
-            out[:, base : base + 32 * blocks] = share[:, shift : shift + 32 * blocks].astype(bf16)
-        else:
-            out[:, base : base + 128] = share.astype(bf16)
+        turned = lax.dot_general(
+            share.astype(bf16), select[...], (((0,), (0,)), ((), ())), preferred_element_type=f32
+        ).astype(bf16)
+        for b in range(blocks):
+            for i4 in range(4):
+                lags = turned[b * CH : (b + 1) * CH, i4 * 128 : i4 * 128 + LAGS]
+                out[region * 17 + start + b, i4] = lags
 
     adding = {}
 
@@ -382,8 +385,8 @@
         copy = pltpu.make_async_remote_copy(
             src_ref=src,
             dst_ref=dst,
-            send_sem=r_send.at[k * 3 + n],
-            recv_sem=r_recv.at[k * 3 + n],
+            send_sem=r_send.at[k * 4 + n],
+            recv_sem=r_recv.at[k * 4 + n],
             device_id=at_band(to),
             device_id_type=MESH,
         )
@@ -393,6 +396,7 @@
     odd = lax.rem(zh, 2)
     mate, beyond, far = zh + 1 - 2 * odd, lax.rem(zh + 2 * odd + 3, 4), lax.rem(zh + 2, 4)
     to_sibling, to_mate, to_beyond = 2 * zh + 1 - core, 2 * mate + core, 2 * beyond + core
+    to_far = 2 * far + core
 
     def r0(k):
         compute(k)
@@ -406,29 +410,54 @@
         def both(n):
             return parts[k, core, n, :rows].astype(f32) + theirs[k, n, :rows].astype(f32)
 
-        pair_out[k, 0, :rows] = both(mate).astype(bf16)
-        pair_out[k, 1, :rows] = both(far).astype(bf16)
         cut = pl.ds(0, rows)
-        send("pair", 1, k, pair_out.at[k, :, cut], pair_in.at[k, :, cut], to_mate)
-        outer[k, :rows] = both(beyond).astype(bf16)
+        if k in DIRECT:
+            pair_out[k, 1, :rows] = both(far).astype(bf16)
+            send("far", 3, k, pair_out.at[k, 1, cut], final.at[k, 1, cut], to_far)
+            pair_out[k, 0, :rows] = both(mate).astype(bf16)
+            send("pair", 1, k, pair_out.at[k, 0, cut], pair_in.at[k, 0, cut], to_mate)
+            outer[k, :rows] = both(beyond).astype(bf16)
+            send("out", 2, k, outer.at[k, cut], final.at[k, 0, cut], to_beyond)
+        else:
+            pair_out[k, 0, :rows] = both(mate).astype(bf16)
+            pair_out[k, 1, :rows] = both(far).astype(bf16)
+            send("pair", 1, k, pair_out.at[k, :, cut], pair_in.at[k, :, cut], to_mate)
+            outer[k, :rows] = both(beyond).astype(bf16)
         mine[k, :rows] = both(zh).astype(bf16)
 
     def r2(k):
         rows = PACKED[CHUNKS[k][1]]
         adding[("pair", k)].wait_recv()
-        outer[k, :rows] = (outer[k, :rows].astype(f32) + pair_in[k, 1, :rows].astype(f32)).astype(bf16)
-        send("out", 2, k, outer.at[k, pl.ds(0, rows)], final.at[k, pl.ds(0, rows)], to_beyond)
+        if k not in DIRECT:
+            passed = outer[k, :rows].astype(f32) + pair_in[k, 1, :rows].astype(f32)
+            outer[k, :rows] = passed.astype(bf16)
+            send("out", 2, k, outer.at[k, pl.ds(0, rows)], final.at[k, 0, pl.ds(0, rows)], to_beyond)
         place(k, 0, mine[k, :rows].astype(f32) + pair_in[k, 0, :rows].astype(f32))
 
     def r3(k):
         rows = PACKED[CHUNKS[k][1]]
         adding[("out", k)].wait_recv()
-        place(k, 1, final[k, :rows].astype(f32))
+        whole = final[k, 0, :rows].astype(f32)
+        if k in DIRECT:
+            adding[("far", k)].wait_recv()
+            whole = whole + final[k, 1, :rows].astype(f32)
+        place(k, 1, whole)
 
     kt_copy.wait()
-    out[:, 17 * CH : REGION] = jnp.zeros((PART, REGION - 17 * CH), bf16)
-    out[:, REGION + 17 * CH :] = jnp.zeros((PART, REGION - 17 * CH), bf16)
+    select_copy.wait()
     stages = {"c": r0, "s": r1, "m": r2, "f": r3}
+    arrive(8, 0)
+
+    @pl.when(first == 1)
+    def _():
+        arrive(8, 1)
+        arrive(1, 0)
+
+    @pl.when(first == 0)
+    def _():
+        arrive(1, 0)
+        arrive(8, 1)
+
     for step in STEPS:
         if step[0] in stages:
             stages[step[0]](int(step[1:]))
@@ -443,24 +472,20 @@
         copy.wait_send()
 
 
-def _place_kernel(table, place, summed, select, out, turned):
+def _place_kernel(table, place, turned, out, sems):
     tile = lax.axis_index("tile")
     side = lax.axis_index("band") // 4
-    rows = lax.dot_general(
-        summed[...], select[...], (((0,), (0,)), ((), ())), preferred_element_type=jnp.float32
-    )
-    turned[...] = rows.astype(jnp.bfloat16).reshape(turned.shape)
-
-    def step(s, carry):
+
+    def copy(s):
         partner = table[0, s]
         behind = lax.rem(tile // 2 - partner // 2 + TILE // 2, TILE // 2)
-        other = lax.rem(partner + side, 2)
-        block = place[behind] + other * (REGION // CH)
-        for i4 in range(4):
-            out[s, i4] = turned[block, :, i4 * 128 : i4 * 128 + LAGS]
-        return carry
-
-    lax.fori_loop(0, out.shape[0], step, 0)
+        block = place[behind] + lax.rem(partner + side, 2) * 17
+        return pltpu.make_async_copy(turned.at[block], out.at[s], sems.at[s])
+
+    for s in range(out.shape[0]):
+        copy(s).start()
+    for s in range(out.shape[0]):
+        copy(s).wait()
 
 
 def body(waveforms, band_widths, pair_table):
@@ -472,7 +497,7 @@
         pltpu.VMEM((BINGROUPS * ROWS, SAMPLES), bf16),
         pltpu.VMEM((BINGROUPS, MSG, 128), bf16),
         pltpu.VMEM((2, BAND, MSG, 128), bf16),
-        pltpu.VMEM((17 * CH, WIDE), bf16),
+        pltpu.VMEM((2, 17 * CH, WIDE // 2), bf16),
         pltpu.VMEM((GROUPS, 256, 256), bf16),
         pltpu.VMEM((4 * PART, GROUPS * 128), bf16),
         pltpu.VMEM((GROUPS * 128, 256), bf16),
@@ -482,45 +507,52 @@
         pltpu.VMEM((len(CHUNKS), 2, PART, 128), bf16),
         pltpu.VMEM((len(CHUNKS), 2, PART, 128), bf16),
         pltpu.VMEM((len(CHUNKS), PART, 128), bf16),
-        pltpu.VMEM((len(CHUNKS), PART, 128), bf16),
+        pltpu.VMEM((len(CHUNKS), 2, PART, 128), bf16),
+        pltpu.VMEM((PART, 512), bf16),
     ]
     dma = pltpu.SemaphoreType.DMA
     scratch += [
-        dma((4,)),
+        dma((5,)),
         dma((BAND,)),
         dma((BAND,)),
         dma((BINGROUPS,)),
         dma((BAND,)),
         dma((32,)),
         dma((32,)),
-        dma((3 * len(CHUNKS),)),
-        dma((3 * len(CHUNKS),)),
+        dma((4 * len(CHUNKS),)),
+        dma((4 * len(CHUNKS),)),
     ]
     vmem = pl.BlockSpec(memory_space=pltpu.VMEM)
     smem = pl.BlockSpec(memory_space=pltpu.SMEM)
     summed = pl.pallas_call(
         _main_kernel,
-        out_shape=jax.ShapeDtypeStruct((PART, JALL), bf16),
-        in_specs=[pl.BlockSpec(memory_space=pl.ANY)] * 4,
+        out_shape=jax.ShapeDtypeStruct((34, 4, CH, LAGS), bf16),
+        in_specs=[pl.BlockSpec(memory_space=pl.ANY)] * 5,
         out_specs=vmem,
         scratch_shapes=scratch,
         compiler_params=pltpu.CompilerParams(
             collective_id=0, has_side_effects=True, vmem_limit_bytes=60 * 1024 * 1024
         ),
         name="correlate",
-    )(band_widths, waveforms, jnp.asarray(_forward_const()), jnp.asarray(_inverse_const()))
+    )(
+        band_widths,
+        waveforms,
+        jnp.asarray(_forward_const()),
+        jnp.asarray(_inverse_const()),
+        jnp.asarray(_select_const()),
+    )
     place = np.zeros((TILE // 2,), np.int32)
     for r, i in POS.items():
         place[r] = i
     placed = pl.pallas_call(
         _place_kernel,
         out_shape=jax.ShapeDtypeStruct((slots, 4, CH, LAGS), bf16),
-        in_specs=[smem, smem, vmem, vmem],
-        out_specs=vmem,
-        scratch_shapes=[pltpu.VMEM((JALL // CH, CH, 512), bf16)],
-        compiler_params=pltpu.CompilerParams(vmem_limit_bytes=32 * 1024 * 1024),
+        in_specs=[smem, smem, pl.BlockSpec(memory_space=pl.ANY)],
+        out_specs=pl.BlockSpec(memory_space=pl.ANY),
+        scratch_shapes=[pltpu.SemaphoreType.DMA((slots,))],
+        compiler_params=pltpu.CompilerParams(vmem_limit_bytes=60 * 1024 * 1024),
         name="place",
-    )(pair_table, jnp.asarray(place), summed, jnp.asarray(_select_const()))
+    )(pair_table, jnp.asarray(place), summed)
     return placed[None]
 
 

time: 83.6 us -> 114 us (1.36)
  Pallas kernels: 82 us -> 114 us
    pallas_call x1, Pallas kernels: 3.01 us -> 34.9 us  [body(): pl.pallas_call(_place_kernel, out_shape=jax.ShapeDtypeStruct((slots, 4, C...]
where the time goes in v4:
time: 114 us
  Pallas kernels  114 us (100%)
    pallas_call x1, Pallas kernels, body(): pl.pallas_call(_main_kernel, out_shape=jax.ShapeDtypeStruct((34, 4, CH, L...  79.2 us
    pallas_call x1, Pallas kernels, body(): pl.pallas_call(_place_kernel, out_shape=jax.ShapeDtypeStruct((slots, 4, C...  34.9 us

profile of v4, /device:TPU:1, one launch (start us, length us, event | category | flops | bytes accessed | tf_op | source)
XLA Modules:
  0.0 114.0 jit_solution(15644614472538494787)
XLA Ops:
  0.0 79.2 %correlate.1.turned = bf16[34,4,32,51]{3,2,1,0:T(8,128)(2,1)} custom-call(s32[8]{0:T(128)} %widths_hbm.1, bf16[32,4,500]{2,1,0:T(4,128)(2,1)} %wave_hbm.1, bf16[384,500]{1,0:T(8,128)(2,1)} %constant.8.clone.fwd_hbm, bf16[4,832,1536]{2,1,0:T(8,128)(2,1)} %constant.9.clone.inv_all, bf16[208,512]{1,0:T(8,128)(2,1)} %constant.10.clone.select_hbm), custom_call_target="tpu_custom_call" | custom-call | tf_op jit(solution)/shard_map/correlate/pallas_call | solution.py:527
  79.2 34.9 %place.2 = bf16[33,4,32,51]{3,2,1,0:T(8,128)(2,1)} custom-call(s32[1,33]{1,0:T(1,128)} %table.1, s32[32]{0:T(128)} %constant.11.clone.place, bf16[34,4,32,51]{3,2,1,0:T(8,128)(2,1)} %correlate.1.turned), custom_call_target="tpu_custom_call" | custom-call | tf_op jit(solution)/shard_map/place/pallas_call | solution.py:547

commit v5 on v4

--- a/solution.py
+++ b/solution.py
@@ -84,7 +84,7 @@
 def _main_kernel(widths_hbm, wave_hbm, fwd_hbm, inv_all, select_hbm, out, *scratch):
     widths, wave, fwd, sb, rb, g, wt, kt, ct = scratch[:9]
     parts, theirs, mine, pair_out, pair_in, outer, final, select = scratch[9:17]
-    (in_sem, a_send, a_recv, o_send, o_recv, g_send, g_recv, r_send, r_recv) = scratch[17:]
+    (in_sem, a_send, a_recv, o_recv, g_send, g_recv, r_send, r_recv) = scratch[17:]
     f32, bf16 = jnp.float32, jnp.bfloat16
 
     band = lax.axis_index("band")
@@ -168,32 +168,39 @@
     pl.semaphore_wait(barrier, len(peers) + BINGROUPS)
 
     exchange = []
-    for o in range(1, BAND):
-        to = lax.rem(band + o, BAND)
+
+    def share(n, to, tile_to, which, sems):
+        o = lax.rem(to - band + BAND, BAND)
         copy = pltpu.make_async_remote_copy(
             src_ref=sb.at[lax.rem(to, BINGROUPS)],
-            dst_ref=rb.at[0, o],
-            send_sem=a_send.at[o],
-            recv_sem=a_recv.at[o],
-            device_id=at_band(to),
+            dst_ref=rb.at[which, o],
+            send_sem=a_send.at[n],
+            recv_sem=sems.at[o],
+            device_id={"band": to, "tile": tile_to},
             device_id_type=MESH,
         )
-        copy.start()
-        exchange.append(copy)
-    across = []
+        if which:
+            copy.start()
+        else:
+            pl.when(to != band)(copy.start)
+        exchange.append((to, which, copy))
+
     for j in range(BINGROUPS):
-        to = 4 * z + j
-        o = lax.rem(to - band + BAND, BAND)
-        copy = pltpu.make_async_remote_copy(
-            src_ref=sb.at[j],
-            dst_ref=rb.at[1, o],
-            send_sem=o_send.at[j],
-            recv_sem=o_recv.at[o],
-            device_id={"band": to, "tile": other_z},
-            device_id_type=MESH,
-        )
-        copy.start()
-        across.append(copy)
+        share(j, 4 * z + j, tile, 0, a_recv)
+        share(4 + j, 4 * z + j, other_z, 1, o_recv)
+    for j in range(BINGROUPS):
+        share(8 + j, 4 - 4 * z + j, tile, 0, a_recv)
+
+    def collect(which):
+        for o in range(1 - which, BAND):
+            pltpu.make_async_remote_copy(
+                src_ref=sb.at[0],
+                dst_ref=rb.at[which, o],
+                send_sem=a_send.at[0],
+                recv_sem=(o_recv if which else a_recv).at[o],
+                device_id={"band": band, "tile": other_z},
+                device_id_type=MESH,
+            ).wait_recv()
 
     lane = lax.broadcasted_iota(jnp.int32, (CH, 128), 1)
 
@@ -235,21 +242,8 @@
                 tiles.append([jnp.where(lane < 64, low[2 * v], high[2 * v + 1]) for v in range(2)])
         return tiles
 
-    for copy in exchange:
-        copy.wait_recv()
-
-    @pl.when(jnp.logical_not(home))
-    def _():
-        for o in range(BAND):
-            pltpu.make_async_remote_copy(
-                src_ref=sb.at[0],
-                dst_ref=rb.at[1, o],
-                send_sem=o_send.at[0],
-                recv_sem=o_recv.at[o],
-                device_id={"band": band, "tile": other_z},
-                device_id_type=MESH,
-            ).wait_recv()
-
+    pl.when(home)(lambda: collect(0))
+    pl.when(jnp.logical_not(home))(lambda: collect(1))
     for n, halves in enumerate(whiten(lax.rem(z + side, 2))):
         for v in range(2):
             first_lane = n % (GROUPS // 2) * 256 + v * 128
@@ -324,6 +318,7 @@
 
     even = lax.rem(lane, 2) == 0
     bin4 = lax.rem(lane // 2, 4)
+    pl.when(jnp.logical_not(home))(lambda: collect(0))
     for n, halves in enumerate(whiten(0)):
         for v in range(2):
             own = halves[v]
@@ -464,28 +459,28 @@
         else:
             arrive(int(step[:-1]), "ab".index(step[-1]))
 
-    for copy in exchange + across:
-        copy.wait_send()
+    for to, which, copy in exchange:
+        if which:
+            copy.wait_send()
+        else:
+            pl.when(to != band)(copy.wait_send)
     for copy in copies.values():
         copy.wait_send()
     for copy in adding.values():
         copy.wait_send()
 
 
-def _place_kernel(table, place, turned, out, sems):
+def _place_kernel(table, place, turned, out):
     tile = lax.axis_index("tile")
     side = lax.axis_index("band") // 4
 
-    def copy(s):
+    def step(s, carry):
         partner = table[0, s]
         behind = lax.rem(tile // 2 - partner // 2 + TILE // 2, TILE // 2)
-        block = place[behind] + lax.rem(partner + side, 2) * 17
-        return pltpu.make_async_copy(turned.at[block], out.at[s], sems.at[s])
-
-    for s in range(out.shape[0]):
-        copy(s).start()
-    for s in range(out.shape[0]):
-        copy(s).wait()
+        out[s] = turned[place[behind] + lax.rem(partner + side, 2) * 17]
+        return carry
+
+    lax.fori_loop(0, out.shape[0], step, 0)
 
 
 def body(waveforms, band_widths, pair_table):
@@ -513,9 +508,8 @@
     dma = pltpu.SemaphoreType.DMA
     scratch += [
         dma((5,)),
+        dma((12,)),
         dma((BAND,)),
-        dma((BAND,)),
-        dma((BINGROUPS,)),
         dma((BAND,)),
         dma((32,)),
         dma((32,)),
@@ -547,10 +541,8 @@
     placed = pl.pallas_call(
         _place_kernel,
         out_shape=jax.ShapeDtypeStruct((slots, 4, CH, LAGS), bf16),
-        in_specs=[smem, smem, pl.BlockSpec(memory_space=pl.ANY)],
-        out_specs=pl.BlockSpec(memory_space=pl.ANY),
-        scratch_shapes=[pltpu.SemaphoreType.DMA((slots,))],
-        compiler_params=pltpu.CompilerParams(vmem_limit_bytes=60 * 1024 * 1024),
+        in_specs=[smem, smem, vmem],
+        out_specs=vmem,
         name="place",
     )(pair_table, jnp.asarray(place), summed)
     return placed[None]

time: 114 us -> 79 us (0.69)
  Pallas kernels: 114 us -> 78.8 us
    pallas_call x1, Pallas kernels: 34.9 us -> 3.21 us  [body(): pl.pallas_call(_place_kernel, out_shape=jax.ShapeDtypeStruct((slots, 4, C...]
    pallas_call x1, Pallas kernels: 79.2 us -> 75.6 us  [body(): pl.pallas_call(_main_kernel, out_shape=jax.ShapeDtypeStruct((34, 4, CH, L...]
where the time goes in v5:
time: 79 us; the launch traced here: 78.8 us
  Pallas kernels  78.8 us (100%)
    pallas_call x1, Pallas kernels, body(): pl.pallas_call(_main_kernel, out_shape=jax.ShapeDtypeStruct((34, 4, CH, L...  75.6 us
    pallas_call x1, Pallas kernels, body(): pl.pallas_call(_place_kernel, out_shape=jax.ShapeDtypeStruct((slots, 4, C...  3.21 us

profile of v5, /device:TPU:1, one launch (start us, length us, event | category | flops | bytes accessed | tf_op | source)
XLA Modules:
  0.0 78.8 jit_solution(2237669608314141375)
XLA Ops:
  0.0 75.6 %correlate.1.turned = bf16[34,4,32,51]{3,2,1,0:T(8,128)(2,1)} custom-call(s32[8]{0:T(128)} %widths_hbm.1, bf16[32,4,500]{2,1,0:T(4,128)(2,1)} %wave_hbm.1, bf16[384,500]{1,0:T(8,128)(2,1)} %constant.8.clone.fwd_hbm, bf16[4,832,1536]{2,1,0:T(8,128)(2,1)} %constant.9.clone.inv_all, bf16[208,512]{1,0:T(8,128)(2,1)} %constant.10.clone.select_hbm), custom_call_target="tpu_custom_call" | custom-call | tf_op jit(solution)/shard_map/correlate/pallas_call | solution.py:521
  75.6 3.2 %place.2 = bf16[33,4,32,51]{3,2,1,0:T(8,128)(2,1)} custom-call(s32[1,33]{1,0:T(1,128)} %table.1, s32[32]{0:T(128)} %constant.11.clone.place, bf16[34,4,32,51]{3,2,1,0:T(8,128)(2,1)} %correlate.1.turned), custom_call_target="tpu_custom_call" | custom-call | tf_op jit(solution)/shard_map/place/pallas_call | solution.py:541

commit v6 on v5

--- a/solution.py
+++ b/solution.py
@@ -65,12 +65,12 @@
         table[k, 0] = np.cos(angle)
         table[k, 1] = -np.sin(angle)
     table = table.reshape(BINGROUPS, GROUPS, 4, 2, LAGS)
-    out = np.zeros((BINGROUPS, 4, PART, GROUPS, 4, 2, 16), np.float32)
-    for b4 in range(4):
+    out = np.zeros((BINGROUPS, 2, PART, GROUPS, 4, 2, 8), np.float32)
+    for b2 in range(2):
         for i4 in range(4):
             rows = np.moveaxis(table, -1, 1)
-            out[:, b4, i4 * LAGS : (i4 + 1) * LAGS, :, :, :, b4 * 4 + i4] = rows
-    return out.reshape(BINGROUPS, 4 * PART, GROUPS * 128).astype(ml_dtypes.bfloat16)
+            out[:, b2, i4 * LAGS : (i4 + 1) * LAGS, :, :, :, b2 * 4 + i4] = rows
+    return out.reshape(BINGROUPS, 2 * PART, GROUPS * 64).astype(ml_dtypes.bfloat16)
 
 
 def _select_const():
@@ -324,11 +324,11 @@
             own = halves[v]
             alt = jnp.where(even, pltpu.roll(own, 127, 1), -pltpu.roll(own, 1, 1))
             for q in range(4):
-                for p in range(2):
-                    kept = jnp.where(bin4 == q, own if p == 0 else alt, 0.0).astype(bf16)
-                    for h in range(2):
-                        row = h * 128 + q * 32 + p * 16
-                        wt[n, row : row + 16, v * 128 : (v + 1) * 128] = kept[h * 16 : h * 16 + 16]
+                kept = [jnp.where(bin4 == q, values, 0.0) for values in (own, alt)]
+                for quarter in range(4):
+                    rows = [values[quarter * 8 : quarter * 8 + 8] for values in kept]
+                    row = quarter * 64 + q * 16
+                    wt[n, row : row + 16, v * 128 : (v + 1) * 128] = jnp.concatenate(rows, axis=0).astype(bf16)
 
     wide = lax.broadcasted_iota(jnp.int32, (PART, 128), 1)
 
@@ -340,12 +340,13 @@
             block = g[n // (GROUPS // 2), start * CH : (start + blocks) * CH, low : low + 256]
             block = jnp.concatenate([block] * (4 // blocks), axis=0)
             cross = lax.dot_general(wt[n], block, nt, preferred_element_type=f32).astype(bf16)
-            for h in range(2):
-                ct[n * 128 : (n + 1) * 128, h * 128 : (h + 1) * 128] = cross[h * 128 : (h + 1) * 128]
+            for quarter in range(4):
+                lanes = slice(quarter * 128, (quarter + 1) * 128)
+                ct[n * 64 : (n + 1) * 64, lanes] = cross[quarter * 64 : (quarter + 1) * 64]
         lags = jnp.dot(kt[...], ct[...], preferred_element_type=f32) * SCALE
-        for h in range(2):
-            for b4 in range(4):
-                share = lags[b4 * PART : (b4 + 1) * PART, h * 128 : (h + 1) * 128]
+        for quarter in range(4):
+            for b2 in range(2):
+                share = lags[b2 * PART : (b2 + 1) * PART, quarter * 128 : (quarter + 1) * 128]
                 if blocks < 4:
                     copies_of = 4 // blocks
                     step = (PART - rows) // (copies_of - 1)
@@ -354,7 +355,7 @@
                         here = wide[:rows] // (32 * blocks) == i
                         packed = jnp.where(here, share[i * step : i * step + rows], packed)
                     share = packed
-                parts[k, b4 % 2, 2 * h + b4 // 2, :rows] = share.astype(bf16)
+                parts[k, b2, quarter, :rows] = share.astype(bf16)
 
     def place(k, region, share):
         start, blocks = CHUNKS[k]
@@ -494,8 +495,8 @@
         pltpu.VMEM((2, BAND, MSG, 128), bf16),
         pltpu.VMEM((2, 17 * CH, WIDE // 2), bf16),
         pltpu.VMEM((GROUPS, 256, 256), bf16),
-        pltpu.VMEM((4 * PART, GROUPS * 128), bf16),
-        pltpu.VMEM((GROUPS * 128, 256), bf16),
+        pltpu.VMEM((2 * PART, GROUPS * 64), bf16),
+        pltpu.VMEM((GROUPS * 64, 512), bf16),
         pltpu.VMEM((len(CHUNKS), 2, 4, PART, 128), bf16),
         pltpu.VMEM((len(CHUNKS), 4, PART, 128), bf16),
         pltpu.VMEM((len(CHUNKS), PART, 128), bf16),

time: 79 us -> 77.4 us (0.980)
  Pallas kernels: 78.8 us -> 77.2 us
    pallas_call x1, Pallas kernels: 75.6 us -> 74 us  [body(): pl.pallas_call(_main_kernel, out_shape=jax.ShapeDtypeStruct((34, 4, CH, L...]
where the time goes in v6:
time: 77.4 us; the launch traced here: 77.2 us
  Pallas kernels  77.2 us (100%)
    pallas_call x1, Pallas kernels, body(): pl.pallas_call(_main_kernel, out_shape=jax.ShapeDtypeStruct((34, 4, CH, L...  74 us
    pallas_call x1, Pallas kernels, body(): pl.pallas_call(_place_kernel, out_shape=jax.ShapeDtypeStruct((slots, 4, C...  3.21 us

profile of v6, /device:TPU:1, one launch (start us, length us, event | category | flops | bytes accessed | tf_op | source)
XLA Modules:
  0.0 77.2 jit_solution(3194686394303559228)
XLA Ops:
  0.0 74.0 %correlate.1.turned = bf16[34,4,32,51]{3,2,1,0:T(8,128)(2,1)} custom-call(s32[8]{0:T(128)} %widths_hbm.1, bf16[32,4,500]{2,1,0:T(4,128)(2,1)} %wave_hbm.1, bf16[384,500]{1,0:T(8,128)(2,1)} %constant.8.clone.fwd_hbm, bf16[4,416,768]{2,1,0:T(8,128)(2,1)} %constant.9.clone.inv_all, bf16[208,512]{1,0:T(8,128)(2,1)} %constant.10.clone.select_hbm), custom_call_target="tpu_custom_call" | custom-call | tf_op jit(solution)/shard_map/correlate/pallas_call | solution.py:522
  74.0 3.2 %place.2 = bf16[33,4,32,51]{3,2,1,0:T(8,128)(2,1)} custom-call(s32[1,33]{1,0:T(1,128)} %table.1, s32[32]{0:T(128)} %constant.11.clone.place, bf16[34,4,32,51]{3,2,1,0:T(8,128)(2,1)} %correlate.1.turned), custom_call_target="tpu_custom_call" | custom-call | tf_op jit(solution)/shard_map/place/pallas_call | solution.py:542

commit v7 on v6

--- a/solution.py
+++ b/solution.py
@@ -35,7 +35,7 @@
 POS = {r: i for i, r in enumerate(ORDER)}
 CHUNKS = [(0, 4), (4, 4), (8, 4), (12, 2), (14, 2), (16, 1)]
 PACKED = {4: PART, 2: 112, 1: 64}
-DIRECT = (4, 5)
+DIRECT = (3, 4, 5)
 STEPS = [
     "1b", "7a", "9a", "16a", "16b", "7b", "9b", "c0",
     "2a", "15a", "s0", "2b", "15b", "10a", "10b", "6a", "c1",

time: 77.4 us -> 78.3 us (1.012)
  Pallas kernels: 77.2 us -> 78.2 us
    pallas_call x1, Pallas kernels: 74 us -> 75 us  [body(): pl.pallas_call(_main_kernel, out_shape=jax.ShapeDtypeStruct((34, 4, CH, L...]
where the time goes in v7:
time: 78.3 us; the launch traced here: 78.2 us
  Pallas kernels  78.2 us (100%)
    pallas_call x1, Pallas kernels, body(): pl.pallas_call(_main_kernel, out_shape=jax.ShapeDtypeStruct((34, 4, CH, L...  75 us
    pallas_call x1, Pallas kernels, body(): pl.pallas_call(_place_kernel, out_shape=jax.ShapeDtypeStruct((slots, 4, C...  3.21 us

profile of v7, /device:TPU:1, one launch (start us, length us, event | category | flops | bytes accessed | tf_op | source)
XLA Modules:
  0.0 78.2 jit_solution(10033007749687616569)
XLA Ops:
  0.0 75.0 %correlate.1.turned = bf16[34,4,32,51]{3,2,1,0:T(8,128)(2,1)} custom-call(s32[8]{0:T(128)} %widths_hbm.1, bf16[32,4,500]{2,1,0:T(4,128)(2,1)} %wave_hbm.1, bf16[384,500]{1,0:T(8,128)(2,1)} %constant.8.clone.fwd_hbm, bf16[4,416,768]{2,1,0:T(8,128)(2,1)} %constant.9.clone.inv_all, bf16[208,512]{1,0:T(8,128)(2,1)} %constant.10.clone.select_hbm), custom_call_target="tpu_custom_call" | custom-call | tf_op jit(solution)/shard_map/correlate/pallas_call | solution.py:522
  75.0 3.2 %place.2 = bf16[33,4,32,51]{3,2,1,0:T(8,128)(2,1)} custom-call(s32[1,33]{1,0:T(1,128)} %table.1, s32[32]{0:T(128)} %constant.11.clone.place, bf16[34,4,32,51]{3,2,1,0:T(8,128)(2,1)} %correlate.1.turned), custom_call_target="tpu_custom_call" | custom-call | tf_op jit(solution)/shard_map/place/pallas_call | solution.py:542
